TPU v7x, 512 devices: a whole 4x4x16 slice. The times are simulated.
512 devices in a mesh: ctx: 32 (over z, core), dp: 16 (over x, y).
Axes of the slice: x: 4, y: 4, z: 16, core: 2. Of those that a mesh axis runs over, the one named last changes fastest.
Arguments:
- queries: bfloat16 [65536, 3072], P(('dp', 'ctx')), parts along dimension 0, may hold values from -96 to 96
- key_vectors: bfloat16 [65536, 512], P(('dp', 'ctx')), parts along dimension 0, may hold values from -4 to 4
- value_matrix: bfloat16 [65536, 512], P(('dp', 'ctx')), parts along dimension 0, may hold values from -6 to 6
- out_grad: bfloat16 [65536, 3072], P(('dp', 'ctx')), parts along dimension 0, may hold values from -6 to 6
- clip_lengths: int32 [336], P('dp'), parts along dimension 0, may hold values from 1 to 6, 64 in all
- clip_full: int32 [336], P('dp'), parts along dimension 0, may hold values 0 or 1
Outputs:
- attended: bfloat16 [65536, 3072], P(('dp', 'ctx')), parts along dimension 0
- query_grad: bfloat16 [65536, 3072], P(('dp', 'ctx')), parts along dimension 0
- gradient_of_keys: bfloat16 [65536, 512], P(('dp', 'ctx')), parts along dimension 0
- gradient_of_values: bfloat16 [65536, 512], P(('dp', 'ctx')), parts along dimension 0
There are 16 independent parts, one for each index of `dp`. A program takes and returns all parts, laid end to end along the dimension named above; each array names one. Nothing has to cross between parts.
Inputs may be any that keep to these rules, and one draw needn't show every extreme that they name: `clip_lengths`: clip lengths in mask blocks of 64 tokens; they sum to 64 and the largest is 6.
All inputs are finite; a program needn't handle non-finite values.
Results may differ from a plain program's by a relative error of at most 0.01.
Values may be sent and summed in bfloat16 or wider, within the bound.
A program may use at most 64 MiB of HBM per device.

v0:
```python
import jax
import jax.numpy as jnp
from jax import lax
from jax.sharding import PartitionSpec as P

HEAD_WIDTH = 128
BLOCK = 64
CLIP_DEVS = 3


def passed_along(value, axis, steps):
    count = lax.axis_size(axis)
    first, last = (max(0, -steps), min(count, count - steps))
    return lax.ppermute(value, axis, [(source, source + steps) for source in range(first, last)])


def clip_index(blocks, clip_ends):
    return jnp.sum(
        (blocks[:, None] >= clip_ends[None, :]).astype(jnp.int32), axis=1, dtype=jnp.int32
    )


def per_device(queries, key_vectors, value_matrix, out_grad, clip_lengths, clip_full):
    local_rows = queries.shape[0]
    devices = lax.axis_size("ctx")
    position = lax.axis_index("ctx")
    reach_devs = CLIP_DEVS
    span_rows = (2 * reach_devs + 1) * local_rows
    key_parts = []
    value_parts = []
    for offset in range(-reach_devs, reach_devs + 1):
        if offset == 0:
            near_keys, near_values = (key_vectors, value_matrix)
        else:
            near_keys, near_values = passed_along((key_vectors, value_matrix), "ctx", -offset)
        key_parts.append(near_keys)
        value_parts.append(near_values)
    window_keys = jnp.concatenate(key_parts, axis=0)
    window_values = jnp.concatenate(value_parts, axis=0)
    first_row = (position - reach_devs) * local_rows
    key_pos = first_row + jnp.arange(span_rows, dtype=jnp.int32)
    query_pos = position * local_rows + jnp.arange(local_rows, dtype=jnp.int32)
    clip_ends = jnp.cumsum(clip_lengths, dtype=jnp.int32)
    query_clip = clip_index(query_pos // BLOCK, clip_ends)
    inside = (key_pos >= 0) & (key_pos < devices * local_rows)
    key_clip = jnp.where(inside, clip_index(key_pos // BLOCK, clip_ends), -1)
    clip_count = clip_full.shape[0]
    query_full = jnp.any(
        (query_clip[:, None] == jnp.arange(clip_count, dtype=jnp.int32)[None, :])
        & (clip_full[None, :] > 0),
        axis=1,
    )
    allowed = (query_clip[:, None] == key_clip[None, :]) & (
        query_full[:, None] | ((key_pos // BLOCK)[None, :] <= (query_pos // BLOCK)[:, None])
    )
    kv_heads = key_vectors.shape[1] // HEAD_WIDTH
    group_members = queries.shape[1] // key_vectors.shape[1]
    score_scale = HEAD_WIDTH ** (-0.5)
    attended_parts = []
    query_parts = []
    key_terms = []
    value_terms = []
    for kv_index in range(kv_heads):
        query_block = queries[
            :, kv_index * group_members * HEAD_WIDTH : (kv_index + 1) * group_members * HEAD_WIDTH
        ].reshape(local_rows, group_members, HEAD_WIDTH)
        grad_block = out_grad[
            :, kv_index * group_members * HEAD_WIDTH : (kv_index + 1) * group_members * HEAD_WIDTH
        ].reshape(local_rows, group_members, HEAD_WIDTH)
        key_block = window_keys[:, kv_index * HEAD_WIDTH : (kv_index + 1) * HEAD_WIDTH]
        value_block = window_values[:, kv_index * HEAD_WIDTH : (kv_index + 1) * HEAD_WIDTH]
        scores = (
            jnp.einsum("thd,kd->htk", query_block, key_block, preferred_element_type=jnp.float32)
            * score_scale
        )
        scores = jnp.where(allowed[None], scores, -jnp.inf)
        peak = jnp.max(scores, axis=2, keepdims=True)
        log_total = peak + jnp.log(jnp.sum(jnp.exp(scores - peak), axis=2, keepdims=True))
        probs = jnp.exp(scores - log_total)
        probs_low = probs.astype(jnp.bfloat16)
        attn_block = jnp.einsum(
            "htk,kd->thd", probs_low, value_block, preferred_element_type=jnp.float32
        )
        delta = jnp.sum(grad_block.astype(jnp.float32) * attn_block, axis=2).T
        dprobs = jnp.einsum(
            "thd,kd->htk", grad_block, value_block, preferred_element_type=jnp.float32
        )
        dscores = (probs * (dprobs - delta[:, :, None])).astype(jnp.bfloat16)
        attended_parts.append(
            attn_block.astype(jnp.bfloat16).reshape(local_rows, group_members * HEAD_WIDTH)
        )
        query_term = score_scale * jnp.einsum(
            "htk,kd->thd", dscores, key_block, preferred_element_type=jnp.float32
        )
        query_parts.append(
            query_term.astype(jnp.bfloat16).reshape(local_rows, group_members * HEAD_WIDTH)
        )
        key_terms.append(
            score_scale
            * jnp.einsum("htk,thd->kd", dscores, query_block, preferred_element_type=jnp.float32)
        )
        value_terms.append(
            jnp.einsum("htk,thd->kd", probs_low, grad_block, preferred_element_type=jnp.float32)
        )
    attended = jnp.concatenate(attended_parts, axis=1)
    query_grad = jnp.concatenate(query_parts, axis=1)
    key_window = jnp.concatenate(key_terms, axis=1).astype(jnp.bfloat16)
    value_window = jnp.concatenate(value_terms, axis=1).astype(jnp.bfloat16)
    own_rows = reach_devs * local_rows
    own_keys = lax.optimization_barrier(key_window[own_rows : own_rows + local_rows])
    own_values = lax.optimization_barrier(value_window[own_rows : own_rows + local_rows])
    key_total = own_keys.astype(jnp.float32)
    value_total = own_values.astype(jnp.float32)
    for offset in range(-reach_devs, reach_devs + 1):
        if offset != 0:
            start_row = (offset + reach_devs) * local_rows
            got_keys, got_values = passed_along(
                (
                    key_window[start_row : start_row + local_rows],
                    value_window[start_row : start_row + local_rows],
                ),
                "ctx",
                offset,
            )
            key_total = key_total + got_keys.astype(jnp.float32)
            value_total = value_total + got_values.astype(jnp.float32)
    return (attended, query_grad, key_total.astype(jnp.bfloat16), value_total.astype(jnp.bfloat16))


def solution(mesh):
    return jax.shard_map(
        per_device,
        mesh=mesh,
        in_specs=(
            P(("dp", "ctx"), None),
            P(("dp", "ctx"), None),
            P(("dp", "ctx"), None),
            P(("dp", "ctx"), None),
            P("dp"),
            P("dp"),
        ),
        out_specs=(
            P(("dp", "ctx"), None),
            P(("dp", "ctx"), None),
            P(("dp", "ctx"), None),
            P(("dp", "ctx"), None),
        ),
        check_vma=False,
    )
```

profile of v0, /device:TPU:1, one launch (start us, length us, event | category | flops | bytes accessed | tf_op | source)
XLA Modules:
  0.0 131.4 jit_solution(13710870991035693067)
XLA Ops:
  1.7 1.3 collective-permute-start.5
  3.0 1.3 collective-permute-start.4
  4.3 8.8 %collective-permute-start.3 = (bf16[128,512]{0,1:T(8,128)(2,1)S(1)}, bf16[128,512]{0,1:T(8,128)(2,1)S(1)}, u32[]{:S(2)}, u32[]{:S(2)}) collective-permute-start(bf16[128,512]{0,1:T(8,128)(2,1)S(1)} %copy.122), channel_id=1, source_target_pairs={{16,0},{32,16},{48,32},{64,48},{80,64},{96,80},{112,96},{128,112},... | collective-permute-start | bytes 393224 | tf_op jit(solution)/shard_map/ppermute | solution.py:14
  13.1 4.5 %collective-permute-start.7 = (bf16[128,512]{1,0:T(8,128)(2,1)}, bf16[128,512]{1,0:T(8,128)(2,1)S(1)}, u32[]{:S(2)}, u32[]{:S(2)}) collective-permute-start(bf16[128,512]{1,0:T(8,128)(2,1)} %param.7), channel_id=1, source_target_pairs={{0,32},{16,48},{32,64},{48,80},{64,96},{80,112},{96,128},{112,144}... | collective-permute-start | bytes 393224 | tf_op jit(solution)/shard_map/ppermute | solution.py:14
  17.6 5.1 %collective-permute-start.6 = (bf16[128,512]{1,0:T(8,128)(2,1)}, bf16[128,512]{1,0:T(8,128)(2,1)S(1)}, u32[]{:S(2)}, u32[]{:S(2)}) collective-permute-start(bf16[128,512]{1,0:T(8,128)(2,1)} %param.7), channel_id=1, source_target_pairs={{0,48},{16,64},{32,80},{48,96},{64,112},{80,128},{96,144},{112,160... | collective-permute-start | bytes 393224 | tf_op jit(solution)/shard_map/ppermute | solution.py:14
  25.8 1.3 fusion.47
  28.9 1.9 %collective-permute-start.8 = (bf16[128,512]{1,0:T(8,128)(2,1)S(1)}, bf16[128,512]{1,0:T(8,128)(2,1)S(1)}, u32[]{:S(2)}, u32[]{:S(2)}) collective-permute-start(bf16[128,512]{1,0:T(8,128)(2,1)S(1)} %copy-done.2), channel_id=1, source_target_pairs={{0,16},{16,32},{32,48},{48,64},{64,80},{80,96},{96,112},{112,128},... | collective-permute-start | bytes 393224 | tf_op jit(solution)/shard_map/ppermute | solution.py:14
  30.8 1.3 collective-permute-start.10
  32.7 1.9 %collective-permute-start.9 = (bf16[128,512]{1,0:T(8,128)(2,1)S(1)}, bf16[128,512]{1,0:T(8,128)(2,1)S(1)}, u32[]{:S(2)}, u32[]{:S(2)}) collective-permute-start(bf16[128,512]{1,0:T(8,128)(2,1)S(1)} %copy-done.2), channel_id=1, source_target_pairs={{16,0},{32,16},{48,32},{64,48},{80,64},{96,80},{112,96},{128,112},... | collective-permute-start | bytes 393224 | tf_op jit(solution)/shard_map/ppermute | solution.py:14
  34.7 5.0 %collective-permute-done.9 = bf16[128,512]{1,0:T(8,128)(2,1)S(1)} collective-permute-done((bf16[128,512]{1,0:T(8,128)(2,1)S(1)}, bf16[128,512]{1,0:T(8,128)(2,1)S(1)}, u32[]{:S(2)}, u32[]{:S(2)}) %collective-permute-start.9) | collective-permute-done | bytes 131104 | tf_op jit(solution)/shard_map/ppermute | solution.py:14
  41.0 3.4 %collective-permute-start.1 = (bf16[128,512]{0,1:T(8,128)(2,1)S(1)}, bf16[128,512]{0,1:T(8,128)(2,1)S(1)}, u32[]{:S(2)}, u32[]{:S(2)}) collective-permute-start(bf16[128,512]{0,1:T(8,128)(2,1)S(1)} %copy.122), channel_id=1, source_target_pairs={{0,32},{16,48},{32,64},{48,80},{64,96},{80,112},{96,128},{112,144}... | collective-permute-start | bytes 393224 | tf_op jit(solution)/shard_map/ppermute | solution.py:14
  44.4 3.3 %collective-permute-done.11 = bf16[128,512]{1,0:T(8,128)(2,1)S(1)} collective-permute-done((bf16[128,512]{1,0:T(8,128)(2,1)S(1)}, bf16[128,512]{1,0:T(8,128)(2,1)S(1)}, u32[]{:S(2)}, u32[]{:S(2)}) %collective-permute-start.11) | collective-permute-done | bytes 131104 | tf_op jit(solution)/shard_map/ppermute | solution.py:14
  47.7 4.8 %collective-permute-start = (bf16[128,512]{0,1:T(8,128)(2,1)S(1)}, bf16[128,512]{0,1:T(8,128)(2,1)S(1)}, u32[]{:S(2)}, u32[]{:S(2)}) collective-permute-start(bf16[128,512]{0,1:T(8,128)(2,1)S(1)} %copy.122), channel_id=1, source_target_pairs={{0,48},{16,64},{32,80},{48,96},{64,112},{80,128},{96,144},{112,160... | collective-permute-start | bytes 393224 | tf_op jit(solution)/shard_map/ppermute | solution.py:14
  54.1 1.5 %collective-permute-done = bf16[128,512]{0,1:T(8,128)(2,1)S(1)} collective-permute-done((bf16[128,512]{0,1:T(8,128)(2,1)S(1)}, bf16[128,512]{0,1:T(8,128)(2,1)S(1)}, u32[]{:S(2)}, u32[]{:S(2)}) %collective-permute-start) | collective-permute-done | bytes 131104 | tf_op jit(solution)/shard_map/ppermute | solution.py:14
  55.6 3.6 %collective-permute-start.2 = (bf16[128,512]{0,1:T(8,128)(2,1)S(1)}, bf16[128,512]{0,1:T(8,128)(2,1)S(1)}, u32[]{:S(2)}, u32[]{:S(2)}) collective-permute-start(bf16[128,512]{0,1:T(8,128)(2,1)S(1)} %copy.122), channel_id=1, source_target_pairs={{0,16},{16,32},{32,48},{48,64},{64,80},{80,96},{96,112},{112,128},... | collective-permute-start | bytes 393224 | tf_op jit(solution)/shard_map/ppermute | solution.py:14
  59.3 1.7 %collective-permute-done.2 = bf16[128,512]{0,1:T(8,128)(2,1)S(1)} collective-permute-done((bf16[128,512]{0,1:T(8,128)(2,1)S(1)}, bf16[128,512]{0,1:T(8,128)(2,1)S(1)}, u32[]{:S(2)}, u32[]{:S(2)}) %collective-permute-start.2) | collective-permute-done | bytes 131104 | tf_op jit(solution)/shard_map/ppermute | solution.py:14
  73.0 1.3 multiply_reduce_fusion.3
  79.3 1.7 %copy.142 = bf16[128,768]{1,0:T(8,128)(2,1)} copy(bf16[128,768]{0,1:T(8,128)(2,1)} %bitcast.215) | data formatting | bytes 393216 | tf_op jit(solution)/shard_map/reshape | solution.py:90
  81.1 1.7 %copy.166 = bf16[128,768]{1,0:T(8,128)(2,1)} copy(bf16[128,768]{0,1:T(8,128)(2,1)} %bitcast.216) | data formatting | bytes 393216 | tf_op jit(solution)/shard_map/reshape | solution.py:96
  83.1 6.3 %collective-permute-start.17 = (bf16[128,512]{0,1:T(8,128)(2,1)S(1)}, bf16[128,512]{0,1:T(8,128)(2,1)S(1)}, u32[]{:S(2)}, u32[]{:S(2)}) collective-permute-start(bf16[128,512]{0,1:T(8,128)(2,1)S(1)} %get-tuple-element.24), channel_id=1, source_target_pairs={{0,48},{16,64},{32,80},{48,96},{64,112},{80,128},{96,144},{112,160... | collective-permute-start | bytes 393224 | tf_op jit(solution)/shard_map/ppermute | solution.py:14
  89.4 3.4 %collective-permute-start.16 = (bf16[128,512]{0,1:T(8,128)(2,1)S(1)}, bf16[128,512]{0,1:T(8,128)(2,1)S(1)}, u32[]{:S(2)}, u32[]{:S(2)}) collective-permute-start(bf16[128,512]{0,1:T(8,128)(2,1)S(1)} %get-tuple-element.25), channel_id=1, source_target_pairs={{0,32},{16,48},{32,64},{48,80},{64,96},{80,112},{96,128},{112,144}... | collective-permute-start | bytes 393224 | tf_op jit(solution)/shard_map/ppermute | solution.py:14
  92.8 1.9 %collective-permute-start.15 = (bf16[128,512]{0,1:T(8,128)(2,1)S(1)}, bf16[128,512]{0,1:T(8,128)(2,1)S(1)}, u32[]{:S(2)}, u32[]{:S(2)}) collective-permute-start(bf16[128,512]{0,1:T(8,128)(2,1)S(1)} %get-tuple-element.26), channel_id=1, source_target_pairs={{0,16},{16,32},{32,48},{48,64},{64,80},{80,96},{96,112},{112,128},... | collective-permute-start | bytes 393224 | tf_op jit(solution)/shard_map/ppermute | solution.py:14
  94.7 2.4 %collective-permute-start.14 = (bf16[128,512]{0,1:T(8,128)(2,1)S(1)}, bf16[128,512]{0,1:T(8,128)(2,1)S(1)}, u32[]{:S(2)}, u32[]{:S(2)}) collective-permute-start(bf16[128,512]{0,1:T(8,128)(2,1)S(1)} %get-tuple-element.27), channel_id=1, source_target_pairs={{16,0},{32,16},{48,32},{64,48},{80,64},{96,80},{112,96},{128,112},... | collective-permute-start | bytes 393224 | tf_op jit(solution)/shard_map/ppermute | solution.py:14
  100.0 7.2 %collective-permute-start.23 = (bf16[128,512]{0,1:T(8,128)(2,1)S(1)}, bf16[128,512]{0,1:T(8,128)(2,1)S(1)}, u32[]{:S(2)}, u32[]{:S(2)}) collective-permute-start(bf16[128,512]{0,1:T(8,128)(2,1)S(1)} %get-tuple-element.17), channel_id=1, source_target_pairs={{0,48},{16,64},{32,80},{48,96},{64,112},{80,128},{96,144},{112,160... | collective-permute-start | bytes 393224 | tf_op jit(solution)/shard_map/ppermute | solution.py:14
  107.2 1.3 %pad_maximum_fusion.2 = (bf16[128,3072]{1,0:T(8,128)(2,1)}, bf16[128,3072]{1,0:T(8,128)(2,1)}) fusion(bf16[128,768]{1,0:T(8,128)(2,1)S(1)} %copy.145, bf16[128,768]{1,0:T(8,128)(2,1)S(1)} %copy.144, bf16[128,768]{1,0:T(8,128)(2,1)S(1)} %copy.143, bf16[128,768]{1,0:T(8,128)(2,1)S(1)} %copy-done, bf16[128,768]{1,0:T(8,128)(2,1)S(1)} %copy.169, ...), kind=kLoop, calls=%fused_computation.62 | loop fusion | flops 6291456 | bytes 3145728 | tf_op jit(solution)/shard_map/concatenate | solution.py:105
  108.6 3.6 %collective-permute-start.22 = (bf16[128,512]{0,1:T(8,128)(2,1)S(1)}, bf16[128,512]{0,1:T(8,128)(2,1)S(1)}, u32[]{:S(2)}, u32[]{:S(2)}) collective-permute-start(bf16[128,512]{0,1:T(8,128)(2,1)S(1)} %get-tuple-element.18), channel_id=1, source_target_pairs={{0,32},{16,48},{32,64},{48,80},{64,96},{80,112},{96,128},{112,144}... | collective-permute-start | bytes 393224 | tf_op jit(solution)/shard_map/ppermute | solution.py:14
  112.2 2.6 %collective-permute-start.21 = (bf16[128,512]{0,1:T(8,128)(2,1)S(1)}, bf16[128,512]{0,1:T(8,128)(2,1)S(1)}, u32[]{:S(2)}, u32[]{:S(2)}) collective-permute-start(bf16[128,512]{0,1:T(8,128)(2,1)S(1)} %get-tuple-element.19), channel_id=1, source_target_pairs={{0,16},{16,32},{32,48},{48,64},{64,80},{80,96},{96,112},{112,128},... | collective-permute-start | bytes 393224 | tf_op jit(solution)/shard_map/ppermute | solution.py:14
  114.8 1.9 %collective-permute-start.20 = (bf16[128,512]{0,1:T(8,128)(2,1)S(1)}, bf16[128,512]{0,1:T(8,128)(2,1)S(1)}, u32[]{:S(2)}, u32[]{:S(2)}) collective-permute-start(bf16[128,512]{0,1:T(8,128)(2,1)S(1)} %get-tuple-element.20), channel_id=1, source_target_pairs={{16,0},{32,16},{48,32},{64,48},{80,64},{96,80},{112,96},{128,112},... | collective-permute-start | bytes 393224 | tf_op jit(solution)/shard_map/ppermute | solution.py:14
  116.7 1.3 collective-permute-start.19
  120.3 1.4 %collective-permute-done.20 = bf16[128,512]{0,1:T(8,128)(2,1)S(1)} collective-permute-done((bf16[128,512]{0,1:T(8,128)(2,1)S(1)}, bf16[128,512]{0,1:T(8,128)(2,1)S(1)}, u32[]{:S(2)}, u32[]{:S(2)}) %collective-permute-start.20) | collective-permute-done | bytes 131104 | tf_op jit(solution)/shard_map/ppermute | solution.py:14
  121.7 3.4 %collective-permute-done.19 = bf16[128,512]{0,1:T(8,128)(2,1)S(1)} collective-permute-done((bf16[128,512]{0,1:T(8,128)(2,1)S(1)}, bf16[128,512]{0,1:T(8,128)(2,1)S(1)}, u32[]{:S(2)}, u32[]{:S(2)}) %collective-permute-start.19) | collective-permute-done | bytes 131104 | tf_op jit(solution)/shard_map/ppermute | solution.py:14
  125.0 5.5 %collective-permute-done.18 = bf16[128,512]{0,1:T(8,128)(2,1)S(1)} collective-permute-done((bf16[128,512]{0,1:T(8,128)(2,1)S(1)}, bf16[128,512]{0,1:T(8,128)(2,1)S(1)}, u32[]{:S(2)}, u32[]{:S(2)}) %collective-permute-start.18) | collective-permute-done | bytes 131104 | tf_op jit(solution)/shard_map/ppermute | solution.py:14
  (107 shorter events, 32.3 us)
Async XLA Ops:
  1.7 59.5 %collective-permute-start.5 = (bf16[128,512]{0,1:T(8,128)(2,1)S(1)}, bf16[128,512]{0,1:T(8,128)(2,1)S(1)}, u32[]{:S(2)}, u32[]{:S(2)}) collective-permute-start(bf16[128,512]{0,1:T(8,128)(2,1)S(1)} %copy.122), channel_id=1, source_target_pairs={{48,0},{64,16},{80,32},{96,48},{112,64},{128,80},{144,96},{160,112... | collective-permute-start | bytes 393224 | tf_op jit(solution)/shard_map/ppermute | solution.py:14
  3.0 58.1 %collective-permute-start.4 = (bf16[128,512]{0,1:T(8,128)(2,1)S(1)}, bf16[128,512]{0,1:T(8,128)(2,1)S(1)}, u32[]{:S(2)}, u32[]{:S(2)}) collective-permute-start(bf16[128,512]{0,1:T(8,128)(2,1)S(1)} %copy.122), channel_id=1, source_target_pairs={{32,0},{48,16},{64,32},{80,48},{96,64},{112,80},{128,96},{144,112}... | collective-permute-start | bytes 393224 | tf_op jit(solution)/shard_map/ppermute | solution.py:14
  4.3 56.8 %collective-permute-start.3 = (bf16[128,512]{0,1:T(8,128)(2,1)S(1)}, bf16[128,512]{0,1:T(8,128)(2,1)S(1)}, u32[]{:S(2)}, u32[]{:S(2)}) collective-permute-start(bf16[128,512]{0,1:T(8,128)(2,1)S(1)} %copy.122), channel_id=1, source_target_pairs={{16,0},{32,16},{48,32},{64,48},{80,64},{96,80},{112,96},{128,112},... | collective-permute-start | bytes 393224 | tf_op jit(solution)/shard_map/ppermute | solution.py:14
  13.1 17.8 %collective-permute-start.7 = (bf16[128,512]{1,0:T(8,128)(2,1)}, bf16[128,512]{1,0:T(8,128)(2,1)S(1)}, u32[]{:S(2)}, u32[]{:S(2)}) collective-permute-start(bf16[128,512]{1,0:T(8,128)(2,1)} %param.7), channel_id=1, source_target_pairs={{0,32},{16,48},{32,64},{48,80},{64,96},{80,112},{96,128},{112,144}... | collective-permute-start | bytes 393224 | tf_op jit(solution)/shard_map/ppermute | solution.py:14
  17.6 11.3 %collective-permute-start.6 = (bf16[128,512]{1,0:T(8,128)(2,1)}, bf16[128,512]{1,0:T(8,128)(2,1)S(1)}, u32[]{:S(2)}, u32[]{:S(2)}) collective-permute-start(bf16[128,512]{1,0:T(8,128)(2,1)} %param.7), channel_id=1, source_target_pairs={{0,48},{16,64},{32,80},{48,96},{64,112},{80,128},{96,144},{112,160... | collective-permute-start | bytes 393224 | tf_op jit(solution)/shard_map/ppermute | solution.py:14
  25.8 3.1 %copy-start.2 = (bf16[128,512]{1,0:T(8,128)(2,1)S(1)}, bf16[128,512]{1,0:T(8,128)(2,1)}, u32[]{:S(2)}) copy-start(bf16[128,512]{1,0:T(8,128)(2,1)} %param.7) | copy-start | bytes 393220
  28.9 3.9 %collective-permute-start.8 = (bf16[128,512]{1,0:T(8,128)(2,1)S(1)}, bf16[128,512]{1,0:T(8,128)(2,1)S(1)}, u32[]{:S(2)}, u32[]{:S(2)}) collective-permute-start(bf16[128,512]{1,0:T(8,128)(2,1)S(1)} %copy-done.2), channel_id=1, source_target_pairs={{0,16},{16,32},{32,48},{48,64},{64,80},{80,96},{96,112},{112,128},... | collective-permute-start | bytes 393224 | tf_op jit(solution)/shard_map/ppermute | solution.py:14
  30.8 10.2 %collective-permute-start.10 = (bf16[128,512]{1,0:T(8,128)(2,1)S(1)}, bf16[128,512]{1,0:T(8,128)(2,1)S(1)}, u32[]{:S(2)}, u32[]{:S(2)}) collective-permute-start(bf16[128,512]{1,0:T(8,128)(2,1)S(1)} %copy-done.2), channel_id=1, source_target_pairs={{32,0},{48,16},{64,32},{80,48},{96,64},{112,80},{128,96},{144,112}... | collective-permute-start | bytes 393224 | tf_op jit(solution)/shard_map/ppermute | solution.py:14
  32.7 7.0 %collective-permute-start.9 = (bf16[128,512]{1,0:T(8,128)(2,1)S(1)}, bf16[128,512]{1,0:T(8,128)(2,1)S(1)}, u32[]{:S(2)}, u32[]{:S(2)}) collective-permute-start(bf16[128,512]{1,0:T(8,128)(2,1)S(1)} %copy-done.2), channel_id=1, source_target_pairs={{16,0},{32,16},{48,32},{64,48},{80,64},{96,80},{112,96},{128,112},... | collective-permute-start | bytes 393224 | tf_op jit(solution)/shard_map/ppermute | solution.py:14
  39.7 8.0 %collective-permute-start.11 = (bf16[128,512]{1,0:T(8,128)(2,1)S(1)}, bf16[128,512]{1,0:T(8,128)(2,1)S(1)}, u32[]{:S(2)}, u32[]{:S(2)}) collective-permute-start(bf16[128,512]{1,0:T(8,128)(2,1)S(1)} %copy-done.2), channel_id=1, source_target_pairs={{48,0},{64,16},{80,32},{96,48},{112,64},{128,80},{144,96},{160,112... | collective-permute-start | bytes 393224 | tf_op jit(solution)/shard_map/ppermute | solution.py:14
  41.0 18.2 %collective-permute-start.1 = (bf16[128,512]{0,1:T(8,128)(2,1)S(1)}, bf16[128,512]{0,1:T(8,128)(2,1)S(1)}, u32[]{:S(2)}, u32[]{:S(2)}) collective-permute-start(bf16[128,512]{0,1:T(8,128)(2,1)S(1)} %copy.122), channel_id=1, source_target_pairs={{0,32},{16,48},{32,64},{48,80},{64,96},{80,112},{96,128},{112,144}... | collective-permute-start | bytes 393224 | tf_op jit(solution)/shard_map/ppermute | solution.py:14
  47.7 7.9 %collective-permute-start = (bf16[128,512]{0,1:T(8,128)(2,1)S(1)}, bf16[128,512]{0,1:T(8,128)(2,1)S(1)}, u32[]{:S(2)}, u32[]{:S(2)}) collective-permute-start(bf16[128,512]{0,1:T(8,128)(2,1)S(1)} %copy.122), channel_id=1, source_target_pairs={{0,48},{16,64},{32,80},{48,96},{64,112},{80,128},{96,144},{112,160... | collective-permute-start | bytes 393224 | tf_op jit(solution)/shard_map/ppermute | solution.py:14
  55.6 5.3 %collective-permute-start.2 = (bf16[128,512]{0,1:T(8,128)(2,1)S(1)}, bf16[128,512]{0,1:T(8,128)(2,1)S(1)}, u32[]{:S(2)}, u32[]{:S(2)}) collective-permute-start(bf16[128,512]{0,1:T(8,128)(2,1)S(1)} %copy.122), channel_id=1, source_target_pairs={{0,16},{16,32},{32,48},{48,64},{64,80},{80,96},{96,112},{112,128},... | collective-permute-start | bytes 393224 | tf_op jit(solution)/shard_map/ppermute | solution.py:14
  82.9 24.3 %copy-start = (bf16[128,768]{1,0:T(8,128)(2,1)S(1)}, bf16[128,768]{1,0:T(8,128)(2,1)}, u32[]{:S(2)}) copy-start(bf16[128,768]{1,0:T(8,128)(2,1)} %copy.142) | copy-start | bytes 589828
  82.9 24.3 %copy-start.1 = (bf16[128,768]{1,0:T(8,128)(2,1)S(1)}, bf16[128,768]{1,0:T(8,128)(2,1)}, u32[]{:S(2)}) copy-start(bf16[128,768]{1,0:T(8,128)(2,1)} %copy.166) | copy-start | bytes 589828
  83.1 15.6 %collective-permute-start.17 = (bf16[128,512]{0,1:T(8,128)(2,1)S(1)}, bf16[128,512]{0,1:T(8,128)(2,1)S(1)}, u32[]{:S(2)}, u32[]{:S(2)}) collective-permute-start(bf16[128,512]{0,1:T(8,128)(2,1)S(1)} %get-tuple-element.24), channel_id=1, source_target_pairs={{0,48},{16,64},{32,80},{48,96},{64,112},{80,128},{96,144},{112,160... | collective-permute-start | bytes 393224 | tf_op jit(solution)/shard_map/ppermute | solution.py:14
  89.4 10.6 %collective-permute-start.16 = (bf16[128,512]{0,1:T(8,128)(2,1)S(1)}, bf16[128,512]{0,1:T(8,128)(2,1)S(1)}, u32[]{:S(2)}, u32[]{:S(2)}) collective-permute-start(bf16[128,512]{0,1:T(8,128)(2,1)S(1)} %get-tuple-element.25), channel_id=1, source_target_pairs={{0,32},{16,48},{32,64},{48,80},{64,96},{80,112},{96,128},{112,144}... | collective-permute-start | bytes 393224 | tf_op jit(solution)/shard_map/ppermute | solution.py:14
  92.8 15.8 %collective-permute-start.15 = (bf16[128,512]{0,1:T(8,128)(2,1)S(1)}, bf16[128,512]{0,1:T(8,128)(2,1)S(1)}, u32[]{:S(2)}, u32[]{:S(2)}) collective-permute-start(bf16[128,512]{0,1:T(8,128)(2,1)S(1)} %get-tuple-element.26), channel_id=1, source_target_pairs={{0,16},{16,32},{32,48},{48,64},{64,80},{80,96},{96,112},{112,128},... | collective-permute-start | bytes 393224 | tf_op jit(solution)/shard_map/ppermute | solution.py:14
  94.7 17.5 %collective-permute-start.14 = (bf16[128,512]{0,1:T(8,128)(2,1)S(1)}, bf16[128,512]{0,1:T(8,128)(2,1)S(1)}, u32[]{:S(2)}, u32[]{:S(2)}) collective-permute-start(bf16[128,512]{0,1:T(8,128)(2,1)S(1)} %get-tuple-element.27), channel_id=1, source_target_pairs={{16,0},{32,16},{48,32},{64,48},{80,64},{96,80},{112,96},{128,112},... | collective-permute-start | bytes 393224 | tf_op jit(solution)/shard_map/ppermute | solution.py:14
  97.1 17.7 %collective-permute-start.13 = (bf16[128,512]{0,1:T(8,128)(2,1)S(1)}, bf16[128,512]{0,1:T(8,128)(2,1)S(1)}, u32[]{:S(2)}, u32[]{:S(2)}) collective-permute-start(bf16[128,512]{0,1:T(8,128)(2,1)S(1)} %get-tuple-element.28), channel_id=1, source_target_pairs={{32,0},{48,16},{64,32},{80,48},{96,64},{112,80},{128,96},{144,112}... | collective-permute-start | bytes 393224 | tf_op jit(solution)/shard_map/ppermute | solution.py:14
  98.7 18.1 %collective-permute-start.12 = (bf16[128,512]{0,1:T(8,128)(2,1)S(1)}, bf16[128,512]{0,1:T(8,128)(2,1)S(1)}, u32[]{:S(2)}, u32[]{:S(2)}) collective-permute-start(bf16[128,512]{0,1:T(8,128)(2,1)S(1)} %get-tuple-element.29), channel_id=1, source_target_pairs={{48,0},{64,16},{80,32},{96,48},{112,64},{128,80},{144,96},{160,112... | collective-permute-start | bytes 393224 | tf_op jit(solution)/shard_map/ppermute | solution.py:14
  100.0 18.1 %collective-permute-start.23 = (bf16[128,512]{0,1:T(8,128)(2,1)S(1)}, bf16[128,512]{0,1:T(8,128)(2,1)S(1)}, u32[]{:S(2)}, u32[]{:S(2)}) collective-permute-start(bf16[128,512]{0,1:T(8,128)(2,1)S(1)} %get-tuple-element.17), channel_id=1, source_target_pairs={{0,48},{16,64},{32,80},{48,96},{64,112},{80,128},{96,144},{112,160... | collective-permute-start | bytes 393224 | tf_op jit(solution)/shard_map/ppermute | solution.py:14
  108.6 11.7 %collective-permute-start.22 = (bf16[128,512]{0,1:T(8,128)(2,1)S(1)}, bf16[128,512]{0,1:T(8,128)(2,1)S(1)}, u32[]{:S(2)}, u32[]{:S(2)}) collective-permute-start(bf16[128,512]{0,1:T(8,128)(2,1)S(1)} %get-tuple-element.18), channel_id=1, source_target_pairs={{0,32},{16,48},{32,64},{48,80},{64,96},{80,112},{96,128},{112,144}... | collective-permute-start | bytes 393224 | tf_op jit(solution)/shard_map/ppermute | solution.py:14
  112.2 8.1 %collective-permute-start.21 = (bf16[128,512]{0,1:T(8,128)(2,1)S(1)}, bf16[128,512]{0,1:T(8,128)(2,1)S(1)}, u32[]{:S(2)}, u32[]{:S(2)}) collective-permute-start(bf16[128,512]{0,1:T(8,128)(2,1)S(1)} %get-tuple-element.19), channel_id=1, source_target_pairs={{0,16},{16,32},{32,48},{48,64},{64,80},{80,96},{96,112},{112,128},... | collective-permute-start | bytes 393224 | tf_op jit(solution)/shard_map/ppermute | solution.py:14
  114.8 6.8 %collective-permute-start.20 = (bf16[128,512]{0,1:T(8,128)(2,1)S(1)}, bf16[128,512]{0,1:T(8,128)(2,1)S(1)}, u32[]{:S(2)}, u32[]{:S(2)}) collective-permute-start(bf16[128,512]{0,1:T(8,128)(2,1)S(1)} %get-tuple-element.20), channel_id=1, source_target_pairs={{16,0},{32,16},{48,32},{64,48},{80,64},{96,80},{112,96},{128,112},... | collective-permute-start | bytes 393224 | tf_op jit(solution)/shard_map/ppermute | solution.py:14
  116.7 8.3 %collective-permute-start.19 = (bf16[128,512]{0,1:T(8,128)(2,1)S(1)}, bf16[128,512]{0,1:T(8,128)(2,1)S(1)}, u32[]{:S(2)}, u32[]{:S(2)}) collective-permute-start(bf16[128,512]{0,1:T(8,128)(2,1)S(1)} %get-tuple-element.21), channel_id=1, source_target_pairs={{32,0},{48,16},{64,32},{80,48},{96,64},{112,80},{128,96},{144,112}... | collective-permute-start | bytes 393224 | tf_op jit(solution)/shard_map/ppermute | solution.py:14
  118.1 12.5 %collective-permute-start.18 = (bf16[128,512]{0,1:T(8,128)(2,1)S(1)}, bf16[128,512]{0,1:T(8,128)(2,1)S(1)}, u32[]{:S(2)}, u32[]{:S(2)}) collective-permute-start(bf16[128,512]{0,1:T(8,128)(2,1)S(1)} %get-tuple-element.22), channel_id=1, source_target_pairs={{48,0},{64,16},{80,32},{96,48},{112,64},{128,80},{144,96},{160,112... | collective-permute-start | bytes 393224 | tf_op jit(solution)/shard_map/ppermute | solution.py:14
where the time goes:
time: 132 us; the launch traced here: 131 us
  starting transfers between devices  73.6 us (56%)
  waiting for transfers between devices  22.4 us (17%)
  matrix products  15.9 us (12%)
  local copies, waits for them, and re-layouts  13.4 us (10%)
  other arithmetic  4.7 us (4%)
  between operations  1.42 us (1%)
    ppermute x24, starting transfers between devices, passed_along(): lax.ppermute(value, axis, [(source, source + steps) for source in range(f...  73.6 us
    ppermute x24, waiting for transfers between devices, passed_along(): lax.ppermute(value, axis, [(source, source + steps) for source in range(f...  22.4 us
    unnamed x25, local copies, waits for them, and re-layouts  3.49 us
    reshape x4, local copies, waits for them, and re-layouts, per_device(): query_term.astype(jnp.bfloat16)  3.32 us
    dot_general x4, matrix products, per_device(): jnp.einsum('htk,kd->thd', probs_low, value_block, preferred_element_type=...  3.18 us
    dot_general x4, matrix products, per_device(): jnp.einsum('htk,kd->thd', dscores, key_block, preferred_element_type=jnp....  2.99 us
    dot_general x4, matrix products, per_device(): jnp.einsum('thd,kd->htk', grad_block, value_block, preferred_element_type...  2.87 us
  transfers between devices with their start and end apart: 24, of which 8 were waited for; matrix products, arithmetic and copies ran while one was open for 8% of the time, Pallas kernels for 0%

commit v1 on v0

v1 whole, which is shorter than its diff:
```python
import jax
import jax.numpy as jnp
from jax import lax
from jax.experimental import pallas as pl
from jax.experimental.pallas import tpu as pltpu
from jax.sharding import PartitionSpec as P

MESH = pl.DeviceIdType.MESH
WIDTH = 128
BLOCK = 64
REACH = 6
CHIP_BLOCKS = 4
WINDOW = CHIP_BLOCKS + 2 * (REACH - 1)
OWN = REACH - 1
LEFT = OWN - CHIP_BLOCKS
RIGHT = OWN + CHIP_BLOCKS
HEADS = 2
SPAN = REACH * BLOCK
LOG2E = 1.4426950408889634


def kernel(
    q_hbm, k_hbm, v_hbm, g_hbm, lengths, fulls,
    o_hbm, dq_hbm, dk_out, dv_out,
    q0, q1, g0, g1, k0, k1, v0, v1, o0, o1, dq0, dq1,
    parts, s0, s1, edge, x0, x1, r0, r1, p0, p1, first, seen,
    kv_send, kv_recv, kv_own, q_own, q_send, q_recv, f_send, f_recv,
    x_send, x_recv, r_send, r_recv, p_send, p_recv, o_own, o_send, o_recv,
):
    q, g, k, v, o, dq = (q0, q1), (g0, g1), (k0, k1), (v0, v1), (o0, o1), (dq0, dq1)
    s, x, r, p = (s0, s1), (x0, x1), (r0, r1), (p0, p1)
    rows = 2 * BLOCK
    group = q0.shape[1] // WIDTH
    cols = group * WIDTH
    me = lax.axis_index("ctx")
    chips = lax.axis_size("ctx") // 2
    chip, core = me // 2, lax.rem(me, 2)
    other = 1 - core
    after = lax.rem(chip + 1, chips)
    before = lax.rem(chip + chips - 1, chips)
    peer = 2 * chip + other

    def away(src, dst, send, recv, target):
        pltpu.make_async_remote_copy(
            src_ref=src, dst_ref=dst, send_sem=send, recv_sem=recv,
            device_id={"ctx": target}, device_id_type=MESH,
        ).start()

    def wait(ref, sem):
        pltpu.make_async_copy(ref, ref, sem).wait()

    def head_columns(head, width):
        return pl.ds(pl.multiple_of(head * width, WIDTH), width)

    barrier = pltpu.get_barrier_semaphore()
    for device in (peer, 2 * before, 2 * before + 1, 2 * after, 2 * after + 1):
        pl.semaphore_signal(barrier, inc=1, device_id={"ctx": device}, device_id_type=MESH)
    pl.semaphore_wait(barrier, 5)

    own_blocks = pl.ds(OWN + 2 * core, 2)
    in_after = pl.ds(LEFT + 2 * core, 2)
    in_before = pl.ds(RIGHT + 2 * core, 2)
    token_rows = pl.ds(pl.multiple_of(core * rows, rows), rows)
    peer_rows = pl.ds(pl.multiple_of(other * rows, rows), rows)

    def send_inputs(h):
        for target in (0, 1):
            head = head_columns(HEADS * target + h, WIDTH)
            for src, dst in ((k_hbm, k[h]), (v_hbm, v[h])):
                away(src.at[:, :, head], dst.at[in_after], kv_send.at[h],
                     kv_recv.at[h, core], 2 * after + target)
                away(src.at[:, :, head], dst.at[in_before], kv_send.at[h],
                     kv_recv.at[h, 2 + core], 2 * before + target)
        mine, theirs = HEADS * core + h, HEADS * other + h
        for src, dst in ((q_hbm, q[h]), (g_hbm, g[h])):
            away(src.at[:, head_columns(theirs, cols)], dst.at[token_rows], q_send.at[h],
                 q_recv.at[h], peer)
        for src, dst in ((k_hbm, k[h]), (v_hbm, v[h])):
            away(src.at[:, :, head_columns(theirs, WIDTH)], dst.at[own_blocks], kv_send.at[h],
                 kv_recv.at[h, 4], peer)
            pltpu.make_async_copy(
                src.at[:, :, head_columns(mine, WIDTH)], dst.at[own_blocks], kv_own.at[h]
            ).start()
        for src, dst in ((q_hbm, q[h]), (g_hbm, g[h])):
            pltpu.make_async_copy(
                src.at[:, head_columns(mine, cols)], dst.at[token_rows], q_own.at[h]
            ).start()

    def forward(h):
        wait(k[h].at[:4], kv_recv.at[h, 1])
        for ref in (k[h], v[h]):
            away(ref.at[OWN - 1], ref.at[0], f_send.at[h], f_recv.at[h, 0], 2 * after + core)
        wait(k[h].at[:4], kv_recv.at[h, 2])
        for ref in (k[h], v[h]):
            away(ref.at[RIGHT], ref.at[WINDOW - 1], f_send.at[h], f_recv.at[h, 1], 2 * before + core)

    def wait_inputs(h):
        wait(q[h], q_own.at[h])
        wait(q[h], q_recv.at[h])
        wait(k[h].at[:4], kv_own.at[h])
        for slot in (0, 3, 4):
            wait(k[h].at[:4], kv_recv.at[h, slot])
        for side in (0, 1):
            wait(k[h].at[:2], f_recv.at[h, side])

    score_scale = WIDTH**-0.5

    def tile(h, t):
        tokens = pl.ds(pl.multiple_of(t * BLOCK, BLOCK), BLOCK)
        begin = first[t]
        count = seen[t]

        def windowed(ref):
            return jnp.concatenate([ref[begin + b] for b in range(REACH)], axis=0)

        keys, values = windowed(k[h]), windowed(v[h])

        def stacked(ref):
            return jnp.concatenate(
                [ref[tokens, pl.ds(m * WIDTH, WIDTH)] for m in range(group)], axis=0
            )

        query, grad = stacked(q[h]), stacked(g[h])
        across = (((1,), (1,)), ((), ()))
        scores = lax.dot_general(keys, query, across, preferred_element_type=jnp.float32)
        logits = [scores[:BLOCK] * (score_scale * LOG2E)]
        for b in range(1, REACH):
            bias = jnp.where(b < count, 0.0, -jnp.inf).astype(jnp.float32)
            logits.append(scores[b * BLOCK : (b + 1) * BLOCK] * (score_scale * LOG2E) + bias)
        logits = jnp.concatenate(logits, axis=0)
        peak = jnp.max(logits, axis=0, keepdims=True)
        weight = jnp.exp2(logits - peak)
        probs = weight * (1.0 / jnp.sum(weight, axis=0, keepdims=True))
        low = probs.astype(jnp.bfloat16)
        down = (((0,), (0,)), ((), ()))
        attn = lax.dot_general(values, low, down, preferred_element_type=jnp.float32)
        dprobs = lax.dot_general(values, grad, across, preferred_element_type=jnp.float32)
        delta = jnp.sum(probs * dprobs, axis=0, keepdims=True)
        dscores = (probs * (dprobs - delta)).astype(jnp.bfloat16)
        dquery = lax.dot_general(keys, dscores, down, preferred_element_type=jnp.float32)
        dkeys = jnp.dot(dscores, query, preferred_element_type=jnp.float32)
        dvalues = jnp.dot(low, grad, preferred_element_type=jnp.float32)
        for b in range(REACH):
            at = slice(b * BLOCK, (b + 1) * BLOCK)
            parts[t, b + 1, :, :WIDTH] = dkeys[at]
            parts[t, b + 1, :, WIDTH:] = dvalues[at]
        attn = attn.astype(jnp.bfloat16).T
        dquery = (dquery * score_scale).astype(jnp.bfloat16).T
        for m in range(group):
            at = pl.ds(m * WIDTH, WIDTH)
            o[h][tokens, at] = attn[m * BLOCK : (m + 1) * BLOCK]
            dq[h][tokens, at] = dquery[m * BLOCK : (m + 1) * BLOCK]

    def tiles(h, start, stop):
        def step(t, carry):
            tile(h, t)
            return carry

        lax.fori_loop(start, stop, step, 0)

    scale_row = jnp.where(
        lax.broadcasted_iota(jnp.int32, (1, 2 * WIDTH), 1) < WIDTH, score_scale, 1.0
    ).astype(jnp.float32)

    def window_sum(w):
        total = None
        for t in range(max(0, w - 2 * OWN), min(CHIP_BLOCKS, w + 1)):
            at = jnp.clip(w - first[t] + 1, 0, REACH + 1)
            term = parts[t, at]
            total = term if total is None else total + term
        return total * scale_row

    def block(w, count=1):
        return pl.ds(w * BLOCK, count * BLOCK)

    def send_partials(h):
        for w, side, target in ((0, 1, before), (WINDOW - 1, 0, after)):
            s[h][block(w), :] = window_sum(w).astype(jnp.bfloat16)
            away(s[h].at[block(w)], x[h].at[side], x_send.at[h], x_recv.at[h, side],
                 2 * target + core)
        for w in (1, 2, 3, 10, 11, 12):
            s[h][block(w), :] = window_sum(w).astype(jnp.bfloat16)
        from_left, from_right = core, 2 + core
        away(s[h].at[block(1, 2)], r[h].at[from_right], r_send.at[h],
             r_recv.at[h, from_right], 2 * before)
        away(s[h].at[block(11, 2)], r[h].at[from_left], r_send.at[h],
             r_recv.at[h, from_left], 2 * after + 1)
        away(s[h].at[block(3)], r[h].at[from_right, pl.ds(0, BLOCK)], r_send.at[h],
             r_recv.at[h, from_right], 2 * before + 1)
        away(s[h].at[block(10)], r[h].at[from_left, pl.ds(BLOCK, BLOCK)], r_send.at[h],
             r_recv.at[h, from_left], 2 * after)
        edge[h, 0] = window_sum(OWN - 1)
        edge[h, 1] = window_sum(RIGHT)
        for w in range(OWN, RIGHT):
            s[h][block(w), :] = window_sum(w).astype(jnp.bfloat16)
        theirs = pl.ds(pl.multiple_of((OWN + 2 * other) * BLOCK, BLOCK), rows)
        away(s[h].at[theirs], p[h], p_send.at[h], p_recv.at[h], peer)

    def send_edges(h):
        from_left, from_right = core, 2 + core
        wait(x[h].at[1], x_recv.at[h, 1])
        s[h][block(OWN - 1), :] = (edge[h, 0] + x[h][1].astype(jnp.float32)).astype(jnp.bfloat16)
        away(s[h].at[block(OWN - 1)], r[h].at[from_right, pl.ds(BLOCK, BLOCK)], r_send.at[h],
             r_recv.at[h, from_right], 2 * before + 1)
        wait(x[h].at[0], x_recv.at[h, 0])
        s[h][block(RIGHT), :] = (edge[h, 1] + x[h][0].astype(jnp.float32)).astype(jnp.bfloat16)
        away(s[h].at[block(RIGHT)], r[h].at[from_left, pl.ds(0, BLOCK)], r_send.at[h],
             r_recv.at[h, from_left], 2 * after)

    def send_outputs(h):
        at = head_columns(HEADS * core + h, cols)
        for src, dst in ((o[h], o_hbm), (dq[h], dq_hbm)):
            away(src.at[peer_rows], dst.at[:, at], o_send.at[h], o_recv.at[h], peer)
            pltpu.make_async_copy(src.at[token_rows], dst.at[:, at], o_own.at[h]).start()

    for h in range(HEADS):
        send_inputs(h)

    zeros = jnp.zeros((BLOCK, 2 * WIDTH), jnp.float32)
    for t in range(CHIP_BLOCKS):
        parts[t, 0] = zeros
        parts[t, REACH + 1] = zeros
    base = chip * CHIP_BLOCKS
    begins, counts = [base + t for t in range(CHIP_BLOCKS)], [1] * CHIP_BLOCKS
    end = jnp.int32(0)
    for i in range(lengths.shape[0]):
        begin, end = end, end + lengths[i]
        for t in range(CHIP_BLOCKS):
            inside = (begin <= base + t) & (base + t < end)
            shown = jnp.where(fulls[i] > 0, end - begin, base + t - begin + 1)
            begins[t] = jnp.where(inside, begin, begins[t])
            counts[t] = jnp.where(inside, shown, counts[t])
    for t in range(CHIP_BLOCKS):
        first[t] = jnp.clip(begins[t] - base + OWN, t, t + OWN)
        seen[t] = counts[t]

    forward(0)
    wait_inputs(0)
    tiles(0, 0, CHIP_BLOCKS - 1)
    forward(1)
    tiles(0, CHIP_BLOCKS - 1, CHIP_BLOCKS)
    send_partials(0)
    send_outputs(0)
    wait_inputs(1)
    tiles(1, 0, 1)
    send_edges(0)
    tiles(1, 1, CHIP_BLOCKS)
    send_partials(1)
    send_outputs(1)
    send_edges(1)

    for h in range(HEADS):
        wait(p[h], p_recv.at[h])
        for slot in range(4):
            wait(r[h].at[slot], r_recv.at[h, slot])
        own_rows = pl.ds(pl.multiple_of((OWN + 2 * core) * BLOCK, BLOCK), rows)
        for source in (0, 1):
            own = jnp.where(core == source, s[h][own_rows, :].astype(jnp.float32),
                            p[h][...].astype(jnp.float32))
            total = own + r[h][source].astype(jnp.float32) + r[h][2 + source].astype(jnp.float32)
            total = total.astype(jnp.bfloat16)
            at = pl.ds((HEADS * source + h) * WIDTH, WIDTH)
            dk_out[:, at] = total[:, :WIDTH]
            dv_out[:, at] = total[:, WIDTH:]

    for h in range(HEADS):
        wait(q[h].at[:, pl.ds(0, 5 * WIDTH)], kv_send.at[h])
        wait(q[h], q_send.at[h])
        wait(k[h].at[:4], f_send.at[h])
        wait(s[h].at[:rows], x_send.at[h])
        wait(s[h].at[: 4 * rows], r_send.at[h])
        wait(p[h], p_send.at[h])
        wait(o[h], o_own.at[h])
        wait(o[h], o_send.at[h])
        wait(o[h], o_recv.at[h])


def per_device(queries, key_vectors, value_matrix, out_grad, clip_lengths, clip_full):
    local, wide = queries.shape
    narrow = key_vectors.shape[1]
    cols = wide // narrow * WIDTH
    low = jnp.bfloat16
    whole = pl.BlockSpec(memory_space=pltpu.HBM)
    scalars = pl.BlockSpec(memory_space=pltpu.SMEM)
    near = pl.BlockSpec(memory_space=pltpu.VMEM)

    def pair(shape, dtype):
        return [pltpu.VMEM(shape, dtype)] * HEADS

    dma = pltpu.SemaphoreType.DMA
    return pl.pallas_call(
        kernel,
        out_shape=(
            jax.ShapeDtypeStruct((local, wide), low),
            jax.ShapeDtypeStruct((local, wide), low),
            jax.ShapeDtypeStruct((local, narrow), low),
            jax.ShapeDtypeStruct((local, narrow), low),
        ),
        in_specs=[whole] * 4 + [scalars] * 2,
        out_specs=(whole, whole, near, near),
        scratch_shapes=[
            *pair((2 * local, cols), low),
            *pair((2 * local, cols), low),
            *pair((WINDOW, BLOCK, WIDTH), low),
            *pair((WINDOW, BLOCK, WIDTH), low),
            *pair((2 * local, cols), low),
            *pair((2 * local, cols), low),
            pltpu.VMEM((CHIP_BLOCKS, REACH + 2, BLOCK, 2 * WIDTH), jnp.float32),
            *pair((WINDOW * BLOCK, 2 * WIDTH), low),
            pltpu.VMEM((HEADS, 2, BLOCK, 2 * WIDTH), jnp.float32),
            *pair((2, BLOCK, 2 * WIDTH), low),
            *pair((4, local, 2 * WIDTH), low),
            *pair((local, 2 * WIDTH), low),
            pltpu.SMEM((CHIP_BLOCKS,), jnp.int32),
            pltpu.SMEM((CHIP_BLOCKS,), jnp.int32),
            dma((HEADS,)), dma((HEADS, 5)), dma((HEADS,)), dma((HEADS,)),
            dma((HEADS,)), dma((HEADS,)), dma((HEADS,)), dma((HEADS, 2)),
            dma((HEADS,)), dma((HEADS, 2)), dma((HEADS,)), dma((HEADS, 4)),
            dma((HEADS,)), dma((HEADS,)), dma((HEADS,)), dma((HEADS,)), dma((HEADS,)),
        ],
        compiler_params=pltpu.CompilerParams(
            collective_id=0, has_side_effects=True, vmem_limit_bytes=56 * 2**20
        ),
        cost_estimate=pl.CostEstimate(
            flops=12 * local * wide * SPAN,
            bytes_accessed=8 * local * (wide + narrow),
            transcendentals=local * wide // WIDTH * SPAN,
        ),
    )(
        queries,
        key_vectors.reshape(-1, BLOCK, narrow),
        value_matrix.reshape(-1, BLOCK, narrow),
        out_grad,
        clip_lengths,
        clip_full,
    )


def solution(mesh):
    sharded = P(("dp", "ctx"), None)
    return jax.shard_map(
        per_device,
        mesh=mesh,
        in_specs=(sharded, sharded, sharded, sharded, P("dp"), P("dp")),
        out_specs=(sharded, sharded, sharded, sharded),
        check_vma=False,
    )
```

time: 132 us -> 45.3 us (0.34)
  the two profiles are of different devices: /device:TPU:1 before, /device:TPU:26 now
where the time goes in v1:
time: 45.3 us; the launch traced here: 45.2 us
  Pallas kernels  39.7 us (88%)
  local copies, waits for them, and re-layouts  4.77 us (11%)
  between operations  0.65 us (1%)
    pallas_call x1, Pallas kernels, per_device(): pl.pallas_call(kernel, out_shape=(jax.ShapeDtypeStruct((local, wide), low...  39.7 us
    unnamed x10, local copies, waits for them, and re-layouts  4.77 us

profile of v1, /device:TPU:26, one launch (start us, length us, event | category | flops | bytes accessed | tf_op | source)
XLA Modules:
  0.0 45.2 jit_solution(1203835223331192533)
XLA Ops:
  0.6 39.7 %shard_map.93 = (bf16[128,3072]{1,0:T(8,128)(2,1)}, bf16[128,3072]{1,0:T(8,128)(2,1)}, bf16[128,512]{1,0:T(8,128)(2,1)}, bf16[128,512]{1,0:T(8,128)(2,1)}) custom-call(bf16[128,3072]{1,0:T(8,128)(2,1)} %q_hbm.1, bf16[2,64,512]{2,1,0:T(8,128)(2,1)} %bitcast.2, bf16[2,64,512]{2,1,0:T(8,128)(2,1)} %bitcast.3, bf16[128,3072]{1,0:T(8,128)(2,1)} %g_hbm.1, ...), custom_call_target="tpu_custom_call" | custom-call | flops 1811939328 | bytes 3670016 | tf_op jit(solution)/shard_map/pallas_call | solution.py:291
  40.4 0.0 copy-start
  40.4 2.1 %copy.14 = bf16[128,3072]{1,0:T(8,128)(2,1)} copy(bf16[128,3072]{1,0:T(8,128)(2,1)} %get-tuple-element.8) | data formatting | bytes 1572864
  42.5 0.0 copy-done
  42.5 0.0 copy-start.2
  42.5 0.9 %copy.15 = bf16[128,3072]{1,0:T(8,128)(2,1)} copy(bf16[128,3072]{1,0:T(8,128)(2,1)S(1)} %copy-done) | data formatting | bytes 1572864
  43.4 0.1 copy-done.2
  43.6 0.0 copy-start.1
  43.6 0.7 %copy.16 = bf16[128,512]{1,0:T(8,128)(2,1)} copy(bf16[128,512]{1,0:T(8,128)(2,1)S(1)} %copy-done.2) | data formatting | bytes 262144
  44.2 0.3 copy-done.1
  44.5 0.7 %copy.17 = bf16[128,512]{1,0:T(8,128)(2,1)} copy(bf16[128,512]{1,0:T(8,128)(2,1)S(1)} %copy-done.1) | data formatting | bytes 262144
Async XLA Ops:
  40.4 2.1 %copy-start = (bf16[128,3072]{1,0:T(8,128)(2,1)S(1)}, bf16[128,3072]{1,0:T(8,128)(2,1)}, u32[]{:S(2)}) copy-start(bf16[128,3072]{1,0:T(8,128)(2,1)} %get-tuple-element.9) | copy-start | bytes 2359300
  42.5 1.0 %copy-start.2 = (bf16[128,512]{1,0:T(8,128)(2,1)S(1)}, bf16[128,512]{1,0:T(8,128)(2,1)}, u32[]{:S(2)}) copy-start(bf16[128,512]{1,0:T(8,128)(2,1)} %get-tuple-element.10) | copy-start | bytes 393220
  43.6 1.0 %copy-start.1 = (bf16[128,512]{1,0:T(8,128)(2,1)S(1)}, bf16[128,512]{1,0:T(8,128)(2,1)}, u32[]{:S(2)}) copy-start(bf16[128,512]{1,0:T(8,128)(2,1)} %get-tuple-element.11) | copy-start | bytes 393220

commit v2 on v1

v2 whole, which is shorter than its diff:
```python
import jax
import jax.numpy as jnp
from jax import lax
from jax.experimental import pallas as pl
from jax.experimental.pallas import tpu as pltpu
from jax.sharding import PartitionSpec as P

MESH = pl.DeviceIdType.MESH
WIDTH = 128
BLOCK = 64
REACH = 6
CHIP_BLOCKS = 4
WINDOW = CHIP_BLOCKS + 2 * (REACH - 1)
OWN = REACH - 1
LEFT = OWN - CHIP_BLOCKS
RIGHT = OWN + CHIP_BLOCKS
HEADS = 2
SPAN = REACH * BLOCK
PIECES = 2
LOG2E = 1.4426950408889634


def kernel(
    q_hbm, k_hbm, v_hbm, g_hbm, lengths, fulls,
    o_hbm, dq_hbm, dk_out, dv_out,
    k_in, v_in, staged, qg_in, qg, kv0, kv1, od, od_far, parts, s0, s1, r0, r1, first, seen,
    kv_in, qg_in_sem, qg_own, kv_send, kv_recv, qg_send, qg_recv,
    r_send, r_recv, o_own, o_send, o_recv, o_far,
):
    kv, s, r = (kv0, kv1), (s0, s1), (r0, r1)
    rows = 2 * BLOCK
    wide = qg.shape[2]
    cols = wide // HEADS
    group = cols // WIDTH
    me, row = lax.axis_index("ctx"), lax.axis_index("dp")
    chips = lax.axis_size("ctx") // 2
    chip, core = me // 2, lax.rem(me, 2)
    other = 1 - core
    after, after2 = (lax.rem(chip + n, chips) for n in (1, 2))
    before, before2 = (lax.rem(chip + chips - n, chips) for n in (1, 2))
    peer = 2 * chip + other

    def away(src, dst, send, recv, target):
        pltpu.make_async_remote_copy(
            src_ref=src, dst_ref=dst, send_sem=send, recv_sem=recv,
            device_id=(target, row), device_id_type=MESH,
        ).start()

    def near(src, dst, sem):
        pltpu.make_async_copy(src, dst, sem).start()

    def wait(ref, sem):
        pltpu.make_async_copy(ref, ref, sem).wait()

    two_off = jnp.where(core == 0, before2, after2)
    barrier = pltpu.get_barrier_semaphore()
    for device in (
        peer, 2 * before, 2 * before + 1, 2 * after, 2 * after + 1,
        2 * two_off, 2 * two_off + 1, jnp.where(core == 0, 2 * after2, 2 * before2 + 1),
    ):
        pl.semaphore_signal(barrier, inc=1, device_id=(device, row), device_id_type=MESH)

    own_blocks = pl.ds(OWN + 2 * core, 2)
    in_after = pl.ds(LEFT + 2 * core, 2)
    in_before = pl.ds(RIGHT + 2 * core, 2)
    token_rows = pl.ds(pl.multiple_of(core * rows, rows), rows)
    peer_rows = pl.ds(pl.multiple_of(other * rows, rows), rows)
    own_rows = pl.ds(pl.multiple_of((OWN + 2 * core) * BLOCK, BLOCK), rows)
    their_rows = pl.ds(pl.multiple_of((OWN + 2 * other) * BLOCK, BLOCK), rows)
    mine = pl.ds(pl.multiple_of(core * wide, WIDTH), wide)
    theirs = pl.ds(pl.multiple_of(other * wide, WIDTH), wide)

    def head_lanes(h):
        return pl.ds(h * cols, cols)

    def send_kv(h):
        for target in (0, 1):
            src = staged.at[HEADS * target + h]
            away(src, kv[h].at[:, in_after], kv_send.at[h], kv_recv.at[h], 2 * after + target)
            away(src, kv[h].at[:, in_before], kv_send.at[h], kv_recv.at[h], 2 * before + target)
            away(src.at[:, core], kv[h].at[:, (WINDOW - 1) * other], kv_send.at[h],
                 kv_recv.at[h], 2 * two_off + target)
        away(staged.at[HEADS * other + h], kv[h].at[:, own_blocks], kv_send.at[h],
             kv_recv.at[h], peer)

    def send_queries(h):
        away(qg_in.at[:, :, head_lanes(h)], qg.at[:, token_rows, head_lanes(h)],
             qg_send, qg_recv.at[h], peer)

    def wait_inputs(h):
        wait(qg.at[:, :rows, head_lanes(h)], qg_recv.at[h])
        wait(kv[h].at[:, : WINDOW - 2], kv_recv.at[h])

    score_scale = WIDTH**-0.5
    across = (((1,), (1,)), ((), ()))
    down = (((0,), (0,)), ((), ()))

    def load(h, t):
        begin = first[t]
        tokens = pl.ds(t * BLOCK, BLOCK)

        def windowed(kind):
            return jnp.concatenate([kv[h][kind, begin + b] for b in range(REACH)], axis=0)

        def stacked(kind):
            return jnp.concatenate(
                [qg[kind, tokens, pl.ds(h * cols + m * WIDTH, WIDTH)] for m in range(group)],
                axis=0,
            )

        return windowed(0), windowed(1), stacked(0), stacked(1)

    def products(h, t):
        keys, values, query, grad = load(h, t)
        scores = lax.dot_general(keys, query, across, preferred_element_type=jnp.float32)
        dprobs = lax.dot_general(values, grad, across, preferred_element_type=jnp.float32)
        return scores, dprobs

    def softmax(t, scores, dprobs):
        count = seen[t]
        bias = [jnp.where(b < count, 0.0, -jnp.inf).astype(jnp.float32) for b in range(REACH)]
        lows, dlows = [], []
        for c in range(scores.shape[1] // WIDTH):
            lanes = slice(c * WIDTH, (c + 1) * WIDTH)
            logits = scores[:, lanes] * (score_scale * LOG2E)
            logits = jnp.concatenate(
                [logits[:BLOCK]]
                + [logits[b * BLOCK : (b + 1) * BLOCK] + bias[b] for b in range(1, REACH)],
                axis=0,
            )
            weight = jnp.exp2(logits - jnp.max(logits, axis=0, keepdims=True))
            probs = weight * (1.0 / jnp.sum(weight, axis=0, keepdims=True))
            lows.append(probs.astype(jnp.bfloat16))
            dprob = dprobs[:, lanes]
            delta = jnp.sum(probs * dprob, axis=0, keepdims=True)
            dlows.append((probs * (dprob - delta)).astype(jnp.bfloat16))
        return jnp.concatenate(lows, axis=1), jnp.concatenate(dlows, axis=1)

    def finish(h, t, low, dscores):
        keys, values, query, grad = load(h, t)
        dkeys = jnp.dot(dscores, query, preferred_element_type=jnp.float32)
        dvalues = jnp.dot(low, grad, preferred_element_type=jnp.float32)
        for b in range(REACH):
            at = slice(b * BLOCK, (b + 1) * BLOCK)
            parts[t, b + 1, :, :WIDTH] = dkeys[at]
            parts[t, b + 1, :, WIDTH:] = dvalues[at]
        attn = lax.dot_general(values, low, down, preferred_element_type=jnp.float32)
        dquery = lax.dot_general(keys, dscores, down, preferred_element_type=jnp.float32)
        attn = attn.astype(jnp.bfloat16).T
        dquery = (dquery * score_scale).astype(jnp.bfloat16).T
        for m in range(group):
            at = pl.ds(h * cols + m * WIDTH, WIDTH)
            tokens = pl.ds(t * BLOCK, BLOCK)
            od[0, tokens, at] = attn[m * BLOCK : (m + 1) * BLOCK]
            od[1, tokens, at] = dquery[m * BLOCK : (m + 1) * BLOCK]

    def tiles(h):
        made = products(h, 0)
        for t in range(CHIP_BLOCKS):
            ready = made
            if t + 1 < CHIP_BLOCKS:
                made = products(h, t + 1)
            finish(h, t, *softmax(t, *ready))

    scale_row = jnp.where(
        lax.broadcasted_iota(jnp.int32, (1, 2 * WIDTH), 1) < WIDTH, score_scale, 1.0
    ).astype(jnp.float32)

    def put_sums(h, *windows):
        for w in windows:
            total = None
            for t in range(max(0, w - 2 * OWN), min(CHIP_BLOCKS, w + 1)):
                term = parts[t, jnp.clip(w - first[t] + 1, 0, REACH + 1)]
                total = term if total is None else total + term
            s[h][pl.ds(w * BLOCK, BLOCK), :] = (total * scale_row).astype(jnp.bfloat16)

    def send_partials(h):
        def part(w, count, slot, target):
            away(s[h].at[pl.ds(w * BLOCK, count * BLOCK)], slot, r_send.at[h], r_recv.at[h],
                 target)

        far = r[h].at[5, pl.ds(pl.multiple_of(core * BLOCK, BLOCK), BLOCK)]
        put_sums(h, 0, WINDOW - 1)
        part(0, 1, far, 2 * before2 + 1)
        part(WINDOW - 1, 1, far, 2 * after2)
        put_sums(h, 1, 2, 9, 10)
        part(LEFT, 2, r[h].at[2 + core], 2 * before)
        part(RIGHT, 2, r[h].at[core], 2 * after)
        put_sums(h, 3, 4, 11, 12)
        part(LEFT + 2, 2, r[h].at[2 + core], 2 * before + 1)
        part(RIGHT + 2, 2, r[h].at[core], 2 * after + 1)
        put_sums(h, *range(OWN, RIGHT))
        away(s[h].at[their_rows], r[h].at[4], r_send.at[h], r_recv.at[h], peer)

    def collect(h):
        wait(r[h], r_recv.at[h])
        nothing = jnp.zeros((BLOCK, 2 * WIDTH), jnp.float32)
        for source in (0, 1):
            own = jnp.where(core == source, s[h][own_rows, :].astype(jnp.float32),
                            r[h][4].astype(jnp.float32))
            far = r[h][5, pl.ds(source * BLOCK, BLOCK)].astype(jnp.float32)
            far = jnp.concatenate(
                [jnp.where(core == 0, far, nothing), jnp.where(core == 1, far, nothing)], axis=0
            )
            total = own + r[h][source].astype(jnp.float32) + r[h][2 + source].astype(jnp.float32)
            total = (total + far).astype(jnp.bfloat16)
            at = pl.ds((HEADS * source + h) * WIDTH, WIDTH)
            dk_out[:, at] = total[:, :WIDTH]
            dv_out[:, at] = total[:, WIDTH:]

    def send_outputs(h):
        away(od.at[:, peer_rows, head_lanes(h)], od_far.at[:, :, head_lanes(h)], o_send,
             o_recv, peer)

    for i, (src, dst) in enumerate(((k_hbm, k_in), (v_hbm, v_in))):
        near(src, dst, kv_in.at[i])
    for i, src in enumerate((q_hbm, g_hbm)):
        near(src.at[:, theirs], qg_in.at[i], qg_in_sem)
        near(src.at[:, mine], qg.at[i, token_rows], qg_own)

    zeros = jnp.zeros((BLOCK, 2 * WIDTH), jnp.float32)
    for t in range(CHIP_BLOCKS):
        parts[t, 0] = zeros
        parts[t, REACH + 1] = zeros
    base = chip * CHIP_BLOCKS
    begins, counts = [base + t for t in range(CHIP_BLOCKS)], [1] * CHIP_BLOCKS
    end = jnp.int32(0)
    for i in range(lengths.shape[0]):
        begin, end = end, end + lengths[i]
        for t in range(CHIP_BLOCKS):
            inside = (begin <= base + t) & (base + t < end)
            shown = jnp.where(fulls[i] > 0, end - begin, base + t - begin + 1)
            begins[t] = jnp.where(inside, begin, begins[t])
            counts[t] = jnp.where(inside, shown, counts[t])
    for t in range(CHIP_BLOCKS):
        first[t] = jnp.clip(begins[t] - base + OWN, t, t + OWN)
        seen[t] = counts[t]

    for kind, held in enumerate((k_in, v_in)):
        wait(held, kv_in.at[kind])
        for head in range(2 * HEADS):
            staged[head, kind] = held[:, :, pl.ds(head * WIDTH, WIDTH)]
    pl.semaphore_wait(barrier, 8)
    send_kv(0)
    wait(qg_in, qg_in_sem)
    send_queries(0)
    send_kv(1)
    send_queries(1)
    for h in range(HEADS):
        for kind in (0, 1):
            kv[h][kind, own_blocks] = staged[HEADS * core + h, kind]
    wait(qg_in, qg_own)

    for h in range(HEADS):
        wait_inputs(h)
        tiles(h)
        send_partials(h)
        send_outputs(h)
    for i, dst in enumerate((o_hbm, dq_hbm)):
        near(od.at[i, token_rows], dst.at[:, mine], o_own)
    collect(0)
    wait(od_far, o_recv)
    for i, dst in enumerate((o_hbm, dq_hbm)):
        near(od_far.at[i], dst.at[:, theirs], o_far)
    collect(1)

    for h in range(HEADS):
        wait(kv[h].at[:, : WINDOW - 2], kv_send.at[h])
        wait(r[h], r_send.at[h])
    wait(qg_in, qg_send)
    wait(od_far, o_send)
    wait(od_far, o_own)
    wait(od_far, o_far)


def settle(*refs):
    refs, (loaded, stored) = refs[:-2], refs[-2:]
    count = len(refs) // 3
    steps = []
    for i in range(count):
        src, dst, held = refs[i], refs[count + i], refs[2 * count + i]
        pieces = PIECES if held.shape == refs[0].shape else 1
        size = held.shape[0] // pieces
        for piece in range(pieces):
            at = pl.ds(piece * size, size)
            load = pltpu.make_async_copy(src.at[at], held.at[at], loaded.at[i, piece])
            store = pltpu.make_async_copy(held.at[at], dst.at[at], stored.at[i, piece])
            load.start()
            steps.append((load, store))
    for load, store in steps:
        load.wait()
        store.start()
    for load, store in steps:
        store.wait()


def per_device(queries, key_vectors, value_matrix, out_grad, clip_lengths, clip_full):
    local, wide = queries.shape
    narrow = key_vectors.shape[1]
    half = wide // 2
    low = jnp.bfloat16
    whole = pl.BlockSpec(memory_space=pltpu.HBM)
    scalars = pl.BlockSpec(memory_space=pltpu.SMEM)
    near = pl.BlockSpec(memory_space=pltpu.VMEM)
    dma = pltpu.SemaphoreType.DMA

    def some(count, shape, dtype=low):
        return [pltpu.VMEM(shape, dtype)] * count

    shapes = [jax.ShapeDtypeStruct((local, n), low) for n in (wide, wide, narrow, narrow)]
    results = pl.pallas_call(
        kernel,
        out_shape=shapes,
        in_specs=[whole] * 4 + [scalars] * 2,
        out_specs=(whole, whole, near, near),
        scratch_shapes=[
            *some(2, (local // BLOCK, BLOCK, narrow)),
            pltpu.VMEM((2 * HEADS, 2, local // BLOCK, BLOCK, WIDTH), low),
            pltpu.VMEM((2, local, half), low),
            pltpu.VMEM((2, 2 * local, half), low),
            *some(HEADS, (2, WINDOW, BLOCK, WIDTH)),
            pltpu.VMEM((2, 2 * local, half), low),
            pltpu.VMEM((2, local, half), low),
            pltpu.VMEM((CHIP_BLOCKS, REACH + 2, BLOCK, 2 * WIDTH), jnp.float32),
            *some(HEADS, (WINDOW * BLOCK, 2 * WIDTH)),
            *some(HEADS, (6, local, 2 * WIDTH)),
            pltpu.SMEM((CHIP_BLOCKS,), jnp.int32),
            pltpu.SMEM((CHIP_BLOCKS,), jnp.int32),
            dma((2,)), dma, dma, dma((HEADS,)), dma((HEADS,)), dma, dma((HEADS,)),
            dma((HEADS,)), dma((HEADS,)), dma, dma, dma, dma,
        ],
        compiler_params=pltpu.CompilerParams(
            collective_id=0, has_side_effects=True, vmem_limit_bytes=56 * 2**20
        ),
        cost_estimate=pl.CostEstimate(
            flops=12 * local * wide * SPAN,
            bytes_accessed=8 * local * (wide + narrow),
            transcendentals=local * wide // WIDTH * SPAN,
        ),
    )(
        queries,
        key_vectors.reshape(-1, BLOCK, narrow),
        value_matrix.reshape(-1, BLOCK, narrow),
        out_grad,
        clip_lengths,
        clip_full,
    )
    return pl.pallas_call(
        settle,
        out_shape=shapes,
        in_specs=[pl.BlockSpec(memory_space=pl.ANY)] * 4,
        out_specs=[whole] * 4,
        scratch_shapes=[
            *some(2, (local, wide)),
            *some(2, (local, narrow)),
            dma((4, PIECES)),
            dma((4, PIECES)),
        ],
        compiler_params=pltpu.CompilerParams(vmem_limit_bytes=56 * 2**20),
    )(*results)


def solution(mesh):
    sharded = P(("dp", "ctx"), None)
    return jax.shard_map(
        per_device,
        mesh=mesh,
        in_specs=(sharded, sharded, sharded, sharded, P("dp"), P("dp")),
        out_specs=(sharded, sharded, sharded, sharded),
        check_vma=False,
    )
```

time: 45.3 us -> 36.5 us (0.81)
  the two profiles are of different devices: /device:TPU:26 before, /device:TPU:1 now
where the time goes in v2:
time: 36.5 us; the launch traced here: 36.3 us
  Pallas kernels  35.6 us (98%)
  between operations  0.64 us (2%)
    pallas_call x1, Pallas kernels, per_device(): pl.pallas_call(kernel, out_shape=shapes, in_specs=[whole] * 4 + [scalars]...  33.3 us
    pallas_call x1, Pallas kernels, per_device(): pl.pallas_call(settle, out_shape=shapes, in_specs=[pl.BlockSpec(memory_sp...  2.35 us

profile of v2, /device:TPU:1, one launch (start us, length us, event | category | flops | bytes accessed | tf_op | source)
XLA Modules:
  0.0 36.3 jit_solution(9356772154347873693)
XLA Ops:
  0.6 33.3 %shard_map.93 = (bf16[128,3072]{1,0:T(8,128)(2,1)}, bf16[128,3072]{1,0:T(8,128)(2,1)}, bf16[128,512]{1,0:T(8,128)(2,1)}, bf16[128,512]{1,0:T(8,128)(2,1)}) custom-call(bf16[128,3072]{1,0:T(8,128)(2,1)} %q_hbm.1, bf16[2,64,512]{2,1,0:T(8,128)(2,1)} %bitcast.2, bf16[2,64,512]{2,1,0:T(8,128)(2,1)} %bitcast.3, bf16[128,3072]{1,0:T(8,128)(2,1)} %g_hbm.1, ...), custom_call_target="tpu_custom_call" | custom-call | flops 1811939328 | bytes 3670016 | tf_op jit(solution)/shard_map/pallas_call | solution.py:311
  33.9 2.4 %shard_map.94 = (bf16[128,3072]{1,0:T(8,128)(2,1)}, bf16[128,3072]{1,0:T(8,128)(2,1)}, bf16[128,512]{1,0:T(8,128)(2,1)}, bf16[128,512]{1,0:T(8,128)(2,1)}) custom-call(bf16[128,3072]{1,0:T(8,128)(2,1)} %get-tuple-element.8.refs_0_, bf16[128,3072]{1,0:T(8,128)(2,1)} %get-tuple-element.9.refs_1_, bf16[128,512]{1,0:T(8,128)(2,1)} %get-tuple-element.10.refs_2_, ...), custom_call_target="tpu_custom_call" | custom-call | tf_op jit(solution)/shard_map/pallas_call | solution.py:348

commit v3 on v2

--- a/solution.py
+++ b/solution.py
@@ -17,13 +17,15 @@
 HEADS = 2
 SPAN = REACH * BLOCK
 PIECES = 2
+ORDER = (0, 3, 1, 2)
 LOG2E = 1.4426950408889634
 
 
 def kernel(
     q_hbm, k_hbm, v_hbm, g_hbm, lengths, fulls,
     o_hbm, dq_hbm, dk_out, dv_out,
-    k_in, v_in, staged, qg_in, qg, kv0, kv1, od, od_far, parts, s0, s1, r0, r1, first, seen,
+    k_in, v_in, staged, qg_in, qg, kv0, kv1, od, od_far, parts, low_held, dlow_held, s0, s1, r0, r1,
+    first, seen,
     kv_in, qg_in_sem, qg_own, kv_send, kv_recv, qg_send, qg_recv,
     r_send, r_recv, o_own, o_send, o_recv, o_far,
 ):
@@ -76,10 +78,10 @@
     def send_kv(h):
         for target in (0, 1):
             src = staged.at[HEADS * target + h]
+            away(src.at[:, core], kv[h].at[:, (WINDOW - 1) * other], kv_send.at[h],
+                 kv_recv.at[h], 2 * two_off + target)
             away(src, kv[h].at[:, in_after], kv_send.at[h], kv_recv.at[h], 2 * after + target)
             away(src, kv[h].at[:, in_before], kv_send.at[h], kv_recv.at[h], 2 * before + target)
-            away(src.at[:, core], kv[h].at[:, (WINDOW - 1) * other], kv_send.at[h],
-                 kv_recv.at[h], 2 * two_off + target)
         away(staged.at[HEADS * other + h], kv[h].at[:, own_blocks], kv_send.at[h],
              kv_recv.at[h], peer)
 
@@ -137,30 +139,42 @@
         return jnp.concatenate(lows, axis=1), jnp.concatenate(dlows, axis=1)
 
     def finish(h, t, low, dscores):
-        keys, values, query, grad = load(h, t)
+        _, _, query, grad = load(h, t)
+        low_held[t] = low
+        dlow_held[t] = dscores
         dkeys = jnp.dot(dscores, query, preferred_element_type=jnp.float32)
         dvalues = jnp.dot(low, grad, preferred_element_type=jnp.float32)
         for b in range(REACH):
             at = slice(b * BLOCK, (b + 1) * BLOCK)
             parts[t, b + 1, :, :WIDTH] = dkeys[at]
             parts[t, b + 1, :, WIDTH:] = dvalues[at]
-        attn = lax.dot_general(values, low, down, preferred_element_type=jnp.float32)
-        dquery = lax.dot_general(keys, dscores, down, preferred_element_type=jnp.float32)
-        attn = attn.astype(jnp.bfloat16).T
-        dquery = (dquery * score_scale).astype(jnp.bfloat16).T
-        for m in range(group):
-            at = pl.ds(h * cols + m * WIDTH, WIDTH)
-            tokens = pl.ds(t * BLOCK, BLOCK)
-            od[0, tokens, at] = attn[m * BLOCK : (m + 1) * BLOCK]
-            od[1, tokens, at] = dquery[m * BLOCK : (m + 1) * BLOCK]
 
     def tiles(h):
-        made = products(h, 0)
+        made = products(h, ORDER[0])
+        for i, t in enumerate(ORDER):
+            ready = made
+            if i + 1 < CHIP_BLOCKS:
+                made = products(h, ORDER[i + 1])
+            finish(h, t, *softmax(t, *ready))
+            if t == 0:
+                put_sums(h, 0)
+                part(h, 0, 1, far_slot(h), 2 * before2 + 1)
+            if t == CHIP_BLOCKS - 1:
+                put_sums(h, WINDOW - 1)
+                part(h, WINDOW - 1, 1, far_slot(h), 2 * after2)
+
+    def outputs(h):
         for t in range(CHIP_BLOCKS):
-            ready = made
-            if t + 1 < CHIP_BLOCKS:
-                made = products(h, t + 1)
-            finish(h, t, *softmax(t, *ready))
+            keys, values, _, _ = load(h, t)
+            attn = lax.dot_general(values, low_held[t], down, preferred_element_type=jnp.float32)
+            dquery = lax.dot_general(keys, dlow_held[t], down, preferred_element_type=jnp.float32)
+            attn = attn.astype(jnp.bfloat16).T
+            dquery = (dquery * score_scale).astype(jnp.bfloat16).T
+            for m in range(group):
+                at = pl.ds(h * cols + m * WIDTH, WIDTH)
+                tokens = pl.ds(t * BLOCK, BLOCK)
+                od[0, tokens, at] = attn[m * BLOCK : (m + 1) * BLOCK]
+                od[1, tokens, at] = dquery[m * BLOCK : (m + 1) * BLOCK]
 
     scale_row = jnp.where(
         lax.broadcasted_iota(jnp.int32, (1, 2 * WIDTH), 1) < WIDTH, score_scale, 1.0
@@ -174,21 +188,19 @@
                 total = term if total is None else total + term
             s[h][pl.ds(w * BLOCK, BLOCK), :] = (total * scale_row).astype(jnp.bfloat16)
 
+    def part(h, w, count, slot, target):
+        away(s[h].at[pl.ds(w * BLOCK, count * BLOCK)], slot, r_send.at[h], r_recv.at[h], target)
+
+    def far_slot(h):
+        return r[h].at[5, pl.ds(pl.multiple_of(core * BLOCK, BLOCK), BLOCK)]
+
     def send_partials(h):
-        def part(w, count, slot, target):
-            away(s[h].at[pl.ds(w * BLOCK, count * BLOCK)], slot, r_send.at[h], r_recv.at[h],
-                 target)
-
-        far = r[h].at[5, pl.ds(pl.multiple_of(core * BLOCK, BLOCK), BLOCK)]
-        put_sums(h, 0, WINDOW - 1)
-        part(0, 1, far, 2 * before2 + 1)
-        part(WINDOW - 1, 1, far, 2 * after2)
         put_sums(h, 1, 2, 9, 10)
-        part(LEFT, 2, r[h].at[2 + core], 2 * before)
-        part(RIGHT, 2, r[h].at[core], 2 * after)
+        part(h, LEFT, 2, r[h].at[2 + core], 2 * before)
+        part(h, RIGHT, 2, r[h].at[core], 2 * after)
         put_sums(h, 3, 4, 11, 12)
-        part(LEFT + 2, 2, r[h].at[2 + core], 2 * before + 1)
-        part(RIGHT + 2, 2, r[h].at[core], 2 * after + 1)
+        part(h, LEFT + 2, 2, r[h].at[2 + core], 2 * before + 1)
+        part(h, RIGHT + 2, 2, r[h].at[core], 2 * after + 1)
         put_sums(h, *range(OWN, RIGHT))
         away(s[h].at[their_rows], r[h].at[4], r_send.at[h], r_recv.at[h], peer)
 
@@ -244,8 +256,6 @@
     send_kv(0)
     wait(qg_in, qg_in_sem)
     send_queries(0)
-    send_kv(1)
-    send_queries(1)
     for h in range(HEADS):
         for kind in (0, 1):
             kv[h][kind, own_blocks] = staged[HEADS * core + h, kind]
@@ -253,8 +263,12 @@
 
     for h in range(HEADS):
         wait_inputs(h)
+        if h + 1 < HEADS:
+            send_kv(h + 1)
+            send_queries(h + 1)
         tiles(h)
         send_partials(h)
+        outputs(h)
         send_outputs(h)
     for i, dst in enumerate((o_hbm, dq_hbm)):
         near(od.at[i, token_rows], dst.at[:, mine], o_own)
@@ -322,6 +336,7 @@
             pltpu.VMEM((2, 2 * local, half), low),
             pltpu.VMEM((2, local, half), low),
             pltpu.VMEM((CHIP_BLOCKS, REACH + 2, BLOCK, 2 * WIDTH), jnp.float32),
+            *some(2, (CHIP_BLOCKS, SPAN, half // HEADS // WIDTH * BLOCK)),
             *some(HEADS, (WINDOW * BLOCK, 2 * WIDTH)),
             *some(HEADS, (6, local, 2 * WIDTH)),
             pltpu.SMEM((CHIP_BLOCKS,), jnp.int32),

time: 36.5 us -> 37.1 us (1.016)
  Pallas kernels: 35.6 us -> 36.3 us
    pallas_call x1, Pallas kernels: 33.3 us -> 33.9 us  [per_device(): pl.pallas_call(kernel, out_shape=shapes, in_specs=[whole] * 4 + [scalars]...]
where the time goes in v3:
time: 37.1 us; the launch traced here: 36.9 us
  Pallas kernels  36.3 us (98%)
  between operations  0.64 us (2%)
    pallas_call x1, Pallas kernels, per_device(): pl.pallas_call(kernel, out_shape=shapes, in_specs=[whole] * 4 + [scalars]...  33.9 us
    pallas_call x1, Pallas kernels, per_device(): pl.pallas_call(settle, out_shape=shapes, in_specs=[pl.BlockSpec(memory_sp...  2.35 us

profile of v3, /device:TPU:1, one launch (start us, length us, event | category | flops | bytes accessed | tf_op | source)
XLA Modules:
  0.0 36.9 jit_solution(17524736563290338981)
XLA Ops:
  0.6 33.9 %shard_map.93 = (bf16[128,3072]{1,0:T(8,128)(2,1)}, bf16[128,3072]{1,0:T(8,128)(2,1)}, bf16[128,512]{1,0:T(8,128)(2,1)}, bf16[128,512]{1,0:T(8,128)(2,1)}) custom-call(bf16[128,3072]{1,0:T(8,128)(2,1)} %q_hbm.1, bf16[2,64,512]{2,1,0:T(8,128)(2,1)} %bitcast.2, bf16[2,64,512]{2,1,0:T(8,128)(2,1)} %bitcast.3, bf16[128,3072]{1,0:T(8,128)(2,1)} %g_hbm.1, ...), custom_call_target="tpu_custom_call" | custom-call | flops 1811939328 | bytes 3670016 | tf_op jit(solution)/shard_map/pallas_call | solution.py:325
  34.6 2.4 %shard_map.94 = (bf16[128,3072]{1,0:T(8,128)(2,1)}, bf16[128,3072]{1,0:T(8,128)(2,1)}, bf16[128,512]{1,0:T(8,128)(2,1)}, bf16[128,512]{1,0:T(8,128)(2,1)}) custom-call(bf16[128,3072]{1,0:T(8,128)(2,1)} %get-tuple-element.8.refs_0_, bf16[128,3072]{1,0:T(8,128)(2,1)} %get-tuple-element.9.refs_1_, bf16[128,512]{1,0:T(8,128)(2,1)} %get-tuple-element.10.refs_2_, ...), custom_call_target="tpu_custom_call" | custom-call | tf_op jit(solution)/shard_map/pallas_call | solution.py:363

commit v4 on v2

--- a/solution.py
+++ b/solution.py
@@ -95,72 +95,108 @@
     across = (((1,), (1,)), ((), ()))
     down = (((0,), (0,)), ((), ()))
 
-    def load(h, t):
+    def windowed(h, kind, t):
         begin = first[t]
+        return jnp.concatenate([kv[h][kind, begin + b] for b in range(REACH)], axis=0)
+
+    def stacked(h, kind, t, members):
         tokens = pl.ds(t * BLOCK, BLOCK)
-
-        def windowed(kind):
-            return jnp.concatenate([kv[h][kind, begin + b] for b in range(REACH)], axis=0)
-
-        def stacked(kind):
-            return jnp.concatenate(
-                [qg[kind, tokens, pl.ds(h * cols + m * WIDTH, WIDTH)] for m in range(group)],
-                axis=0,
-            )
-
-        return windowed(0), windowed(1), stacked(0), stacked(1)
-
-    def products(h, t):
-        keys, values, query, grad = load(h, t)
-        scores = lax.dot_general(keys, query, across, preferred_element_type=jnp.float32)
-        dprobs = lax.dot_general(values, grad, across, preferred_element_type=jnp.float32)
-        return scores, dprobs
-
-    def softmax(t, scores, dprobs):
-        count = seen[t]
-        bias = [jnp.where(b < count, 0.0, -jnp.inf).astype(jnp.float32) for b in range(REACH)]
-        lows, dlows = [], []
-        for c in range(scores.shape[1] // WIDTH):
-            lanes = slice(c * WIDTH, (c + 1) * WIDTH)
-            logits = scores[:, lanes] * (score_scale * LOG2E)
-            logits = jnp.concatenate(
-                [logits[:BLOCK]]
-                + [logits[b * BLOCK : (b + 1) * BLOCK] + bias[b] for b in range(1, REACH)],
-                axis=0,
-            )
-            weight = jnp.exp2(logits - jnp.max(logits, axis=0, keepdims=True))
-            probs = weight * (1.0 / jnp.sum(weight, axis=0, keepdims=True))
-            lows.append(probs.astype(jnp.bfloat16))
-            dprob = dprobs[:, lanes]
-            delta = jnp.sum(probs * dprob, axis=0, keepdims=True)
-            dlows.append((probs * (dprob - delta)).astype(jnp.bfloat16))
-        return jnp.concatenate(lows, axis=1), jnp.concatenate(dlows, axis=1)
-
-    def finish(h, t, low, dscores):
-        keys, values, query, grad = load(h, t)
-        dkeys = jnp.dot(dscores, query, preferred_element_type=jnp.float32)
-        dvalues = jnp.dot(low, grad, preferred_element_type=jnp.float32)
-        for b in range(REACH):
-            at = slice(b * BLOCK, (b + 1) * BLOCK)
-            parts[t, b + 1, :, :WIDTH] = dkeys[at]
-            parts[t, b + 1, :, WIDTH:] = dvalues[at]
-        attn = lax.dot_general(values, low, down, preferred_element_type=jnp.float32)
-        dquery = lax.dot_general(keys, dscores, down, preferred_element_type=jnp.float32)
-        attn = attn.astype(jnp.bfloat16).T
-        dquery = (dquery * score_scale).astype(jnp.bfloat16).T
-        for m in range(group):
-            at = pl.ds(h * cols + m * WIDTH, WIDTH)
-            tokens = pl.ds(t * BLOCK, BLOCK)
-            od[0, tokens, at] = attn[m * BLOCK : (m + 1) * BLOCK]
-            od[1, tokens, at] = dquery[m * BLOCK : (m + 1) * BLOCK]
+        return jnp.concatenate(
+            [qg[kind, tokens, pl.ds(h * cols + m * WIDTH, WIDTH)] for m in members], axis=0
+        )
 
     def tiles(h):
-        made = products(h, 0)
-        for t in range(CHIP_BLOCKS):
-            ready = made
-            if t + 1 < CHIP_BLOCKS:
-                made = products(h, t + 1)
-            finish(h, t, *softmax(t, *ready))
+        work = [
+            (t, members)
+            for t in range(CHIP_BLOCKS)
+            for members in (range(0, 4), range(4, group))
+        ]
+        made, soft, sums = {}, {}, {}
+
+        def products(i):
+            t, members = work[i]
+
+            def step(kind):
+                def run():
+                    made[i, kind] = lax.dot_general(
+                        windowed(h, kind, t), stacked(h, kind, t, members), across,
+                        preferred_element_type=jnp.float32,
+                    )
+
+                return run
+
+            return [step(0), step(1)]
+
+        def softmax(i):
+            t, members = work[i]
+            soft[i] = ([], [])
+
+            def step(c):
+                def run():
+                    count = seen[t]
+                    lanes = slice(c * WIDTH, (c + 1) * WIDTH)
+                    logits = made[i, 0][:, lanes] * (score_scale * LOG2E)
+                    pieces = [logits[:BLOCK]]
+                    for b in range(1, REACH):
+                        bias = jnp.where(b < count, 0.0, -jnp.inf).astype(jnp.float32)
+                        pieces.append(logits[b * BLOCK : (b + 1) * BLOCK] + bias)
+                    logits = jnp.concatenate(pieces, axis=0)
+                    weight = jnp.exp2(logits - jnp.max(logits, axis=0, keepdims=True))
+                    probs = weight * (1.0 / jnp.sum(weight, axis=0, keepdims=True))
+                    soft[i][0].append(probs.astype(jnp.bfloat16))
+                    dprob = made[i, 1][:, lanes]
+                    delta = jnp.sum(probs * dprob, axis=0, keepdims=True)
+                    soft[i][1].append((probs * (dprob - delta)).astype(jnp.bfloat16))
+
+                return run
+
+            return [step(c) for c in range(len(members) * BLOCK // WIDTH)]
+
+        def gradients(i):
+            t, members = work[i]
+
+            def to_keys(kind):
+                def run():
+                    inner = jnp.concatenate(soft[i][1 - kind], axis=1)
+                    sums[i, kind] = jnp.dot(inner, stacked(h, kind, t, members),
+                                            preferred_element_type=jnp.float32)
+                    if i % 2:
+                        total = sums[i - 1, kind] + sums[i, kind]
+                        for b in range(REACH):
+                            parts[t, b + 1, :, pl.ds(kind * WIDTH, WIDTH)] = (
+                                total[b * BLOCK : (b + 1) * BLOCK]
+                            )
+
+                return run
+
+            def to_queries(kind):
+                def run():
+                    inner = jnp.concatenate(soft[i][1 - kind], axis=1)
+                    found = lax.dot_general(windowed(h, kind, t), inner, down,
+                                            preferred_element_type=jnp.float32)
+                    if kind == 0:
+                        found = found * score_scale
+                    found = found.astype(jnp.bfloat16).T
+                    for n, m in enumerate(members):
+                        od[1 - kind, pl.ds(t * BLOCK, BLOCK), pl.ds(h * cols + m * WIDTH, WIDTH)] = (
+                            found[n * BLOCK : (n + 1) * BLOCK]
+                        )
+
+                return run
+
+            return [to_keys(0), to_keys(1), to_queries(0), to_queries(1)]
+
+        for i in range(-1, len(work) + 1):
+            stages = [
+                gradients(i - 1) if 0 < i else [],
+                softmax(i) if 0 <= i < len(work) else [],
+                products(i + 1) if i + 1 < len(work) else [],
+            ]
+            longest = max(len(stage) for stage in stages)
+            for n in range(longest):
+                for stage in stages:
+                    for step in stage[n * len(stage) // longest : (n + 1) * len(stage) // longest]:
+                        step()
 
     scale_row = jnp.where(
         lax.broadcasted_iota(jnp.int32, (1, 2 * WIDTH), 1) < WIDTH, score_scale, 1.0

time: 36.5 us -> 36.7 us (level)
  no operation moved by 1% of the time
where the time goes in v4:
time: 36.7 us; the launch traced here: 36.5 us
  Pallas kernels  35.9 us (98%)
  between operations  0.64 us (2%)
    pallas_call x1, Pallas kernels, per_device(): pl.pallas_call(kernel, out_shape=shapes, in_specs=[whole] * 4 + [scalars]...  33.5 us
    pallas_call x1, Pallas kernels, per_device(): pl.pallas_call(settle, out_shape=shapes, in_specs=[pl.BlockSpec(memory_sp...  2.35 us

profile of v4, /device:TPU:1, one launch (start us, length us, event | category | flops | bytes accessed | tf_op | source)
XLA Modules:
  0.0 36.5 jit_solution(8762267232927977189)
XLA Ops:
  0.6 33.5 %shard_map.93 = (bf16[128,3072]{1,0:T(8,128)(2,1)}, bf16[128,3072]{1,0:T(8,128)(2,1)}, bf16[128,512]{1,0:T(8,128)(2,1)}, bf16[128,512]{1,0:T(8,128)(2,1)}) custom-call(bf16[128,3072]{1,0:T(8,128)(2,1)} %q_hbm.1, bf16[2,64,512]{2,1,0:T(8,128)(2,1)} %bitcast.2, bf16[2,64,512]{2,1,0:T(8,128)(2,1)} %bitcast.3, bf16[128,3072]{1,0:T(8,128)(2,1)} %g_hbm.1, ...), custom_call_target="tpu_custom_call" | custom-call | flops 1811939328 | bytes 3670016 | tf_op jit(solution)/shard_map/pallas_call | solution.py:347
  34.2 2.4 %shard_map.94 = (bf16[128,3072]{1,0:T(8,128)(2,1)}, bf16[128,3072]{1,0:T(8,128)(2,1)}, bf16[128,512]{1,0:T(8,128)(2,1)}, bf16[128,512]{1,0:T(8,128)(2,1)}) custom-call(bf16[128,3072]{1,0:T(8,128)(2,1)} %get-tuple-element.8.refs_0_, bf16[128,3072]{1,0:T(8,128)(2,1)} %get-tuple-element.9.refs_1_, bf16[128,512]{1,0:T(8,128)(2,1)} %get-tuple-element.10.refs_2_, ...), custom_call_target="tpu_custom_call" | custom-call | tf_op jit(solution)/shard_map/pallas_call | solution.py:384

commit v5 on v3

--- a/solution.py
+++ b/solution.py
@@ -260,12 +260,13 @@
         for kind in (0, 1):
             kv[h][kind, own_blocks] = staged[HEADS * core + h, kind]
     wait(qg_in, qg_own)
+    for h in range(1, HEADS):
+        wait(kv[h - 1].at[:, : WINDOW - 2], kv_send.at[h - 1])
+        send_kv(h)
+        send_queries(h)
 
     for h in range(HEADS):
         wait_inputs(h)
-        if h + 1 < HEADS:
-            send_kv(h + 1)
-            send_queries(h + 1)
         tiles(h)
         send_partials(h)
         outputs(h)
@@ -278,8 +279,8 @@
         near(od_far.at[i], dst.at[:, theirs], o_far)
     collect(1)
 
+    wait(kv[HEADS - 1].at[:, : WINDOW - 2], kv_send.at[HEADS - 1])
     for h in range(HEADS):
-        wait(kv[h].at[:, : WINDOW - 2], kv_send.at[h])
         wait(r[h], r_send.at[h])
     wait(qg_in, qg_send)
     wait(od_far, o_send)

time: 37.1 us -> 35.3 us (0.951)
  Pallas kernels: 36.3 us -> 34.5 us
    pallas_call x1, Pallas kernels: 33.9 us -> 32.1 us  [per_device(): pl.pallas_call(kernel, out_shape=shapes, in_specs=[whole] * 4 + [scalars]...]
where the time goes in v5:
time: 35.3 us; the launch traced here: 35.1 us
  Pallas kernels  34.5 us (98%)
  between operations  0.64 us (2%)
    pallas_call x1, Pallas kernels, per_device(): pl.pallas_call(kernel, out_shape=shapes, in_specs=[whole] * 4 + [scalars]...  32.1 us
    pallas_call x1, Pallas kernels, per_device(): pl.pallas_call(settle, out_shape=shapes, in_specs=[pl.BlockSpec(memory_sp...  2.35 us

profile of v5, /device:TPU:1, one launch (start us, length us, event | category | flops | bytes accessed | tf_op | source)
XLA Modules:
  0.0 35.1 jit_solution(2829085482574222441)
XLA Ops:
  0.6 32.1 %shard_map.93 = (bf16[128,3072]{1,0:T(8,128)(2,1)}, bf16[128,3072]{1,0:T(8,128)(2,1)}, bf16[128,512]{1,0:T(8,128)(2,1)}, bf16[128,512]{1,0:T(8,128)(2,1)}) custom-call(bf16[128,3072]{1,0:T(8,128)(2,1)} %q_hbm.1, bf16[2,64,512]{2,1,0:T(8,128)(2,1)} %bitcast.2, bf16[2,64,512]{2,1,0:T(8,128)(2,1)} %bitcast.3, bf16[128,3072]{1,0:T(8,128)(2,1)} %g_hbm.1, ...), custom_call_target="tpu_custom_call" | custom-call | flops 1811939328 | bytes 3670016 | tf_op jit(solution)/shard_map/pallas_call | solution.py:326
  32.8 2.4 %shard_map.94 = (bf16[128,3072]{1,0:T(8,128)(2,1)}, bf16[128,3072]{1,0:T(8,128)(2,1)}, bf16[128,512]{1,0:T(8,128)(2,1)}, bf16[128,512]{1,0:T(8,128)(2,1)}) custom-call(bf16[128,3072]{1,0:T(8,128)(2,1)} %get-tuple-element.8.refs_0_, bf16[128,3072]{1,0:T(8,128)(2,1)} %get-tuple-element.9.refs_1_, bf16[128,512]{1,0:T(8,128)(2,1)} %get-tuple-element.10.refs_2_, ...), custom_call_target="tpu_custom_call" | custom-call | tf_op jit(solution)/shard_map/pallas_call | solution.py:364

commit v6 on v5

--- a/solution.py
+++ b/solution.py
@@ -24,12 +24,12 @@
 def kernel(
     q_hbm, k_hbm, v_hbm, g_hbm, lengths, fulls,
     o_hbm, dq_hbm, dk_out, dv_out,
-    k_in, v_in, staged, qg_in, qg, kv0, kv1, od, od_far, parts, low_held, dlow_held, s0, s1, r0, r1,
+    k_in, v_in, staged, qg_in, qg, kv0, kv1, od, od_far, parts, low_held, dlow_held, s0, s1, x0, x1, r0, r1,
     first, seen,
     kv_in, qg_in_sem, qg_own, kv_send, kv_recv, qg_send, qg_recv,
-    r_send, r_recv, o_own, o_send, o_recv, o_far,
+    x_send, x_recv, r_send, r_recv, o_own, o_send, o_recv, o_far,
 ):
-    kv, s, r = (kv0, kv1), (s0, s1), (r0, r1)
+    kv, s, x, r = (kv0, kv1), (s0, s1), (x0, x1), (r0, r1)
     rows = 2 * BLOCK
     wide = qg.shape[2]
     cols = wide // HEADS
@@ -158,10 +158,12 @@
             finish(h, t, *softmax(t, *ready))
             if t == 0:
                 put_sums(h, 0)
-                part(h, 0, 1, far_slot(h), 2 * before2 + 1)
+                away(s[h].at[pl.ds(0, BLOCK)], x[h].at[1], x_send.at[h], x_recv.at[h, 1],
+                     2 * before + core)
             if t == CHIP_BLOCKS - 1:
                 put_sums(h, WINDOW - 1)
-                part(h, WINDOW - 1, 1, far_slot(h), 2 * after2)
+                away(s[h].at[pl.ds((WINDOW - 1) * BLOCK, BLOCK)], x[h].at[0], x_send.at[h],
+                     x_recv.at[h, 0], 2 * after + core)
 
     def outputs(h):
         for t in range(CHIP_BLOCKS):
@@ -180,42 +182,43 @@
         lax.broadcasted_iota(jnp.int32, (1, 2 * WIDTH), 1) < WIDTH, score_scale, 1.0
     ).astype(jnp.float32)
 
-    def put_sums(h, *windows):
+    def put_sums(h, *windows, more=None):
         for w in windows:
             total = None
             for t in range(max(0, w - 2 * OWN), min(CHIP_BLOCKS, w + 1)):
                 term = parts[t, jnp.clip(w - first[t] + 1, 0, REACH + 1)]
                 total = term if total is None else total + term
-            s[h][pl.ds(w * BLOCK, BLOCK), :] = (total * scale_row).astype(jnp.bfloat16)
-
-    def part(h, w, count, slot, target):
-        away(s[h].at[pl.ds(w * BLOCK, count * BLOCK)], slot, r_send.at[h], r_recv.at[h], target)
-
-    def far_slot(h):
-        return r[h].at[5, pl.ds(pl.multiple_of(core * BLOCK, BLOCK), BLOCK)]
+            total = total * scale_row
+            if more is not None:
+                total = total + more.astype(jnp.float32)
+            s[h][pl.ds(w * BLOCK, BLOCK), :] = total.astype(jnp.bfloat16)
+
+    def part(h, w, slot, target):
+        away(s[h].at[pl.ds(w * BLOCK, 2 * BLOCK)], slot, r_send.at[h], r_recv.at[h], target)
 
     def send_partials(h):
-        put_sums(h, 1, 2, 9, 10)
-        part(h, LEFT, 2, r[h].at[2 + core], 2 * before)
-        part(h, RIGHT, 2, r[h].at[core], 2 * after)
-        put_sums(h, 3, 4, 11, 12)
-        part(h, LEFT + 2, 2, r[h].at[2 + core], 2 * before + 1)
-        part(h, RIGHT + 2, 2, r[h].at[core], 2 * after + 1)
+        put_sums(h, 1, 2, 11, 12)
+        part(h, LEFT, r[h].at[2 + core], 2 * before)
+        part(h, RIGHT + 2, r[h].at[core], 2 * after + 1)
         put_sums(h, *range(OWN, RIGHT))
         away(s[h].at[their_rows], r[h].at[4], r_send.at[h], r_recv.at[h], peer)
+        put_sums(h, 3, 10)
+
+    def send_edges(h):
+        wait(x[h].at[1], x_recv.at[h, 1])
+        put_sums(h, OWN - 1, more=x[h][1])
+        part(h, LEFT + 2, r[h].at[2 + core], 2 * before + 1)
+        wait(x[h].at[0], x_recv.at[h, 0])
+        put_sums(h, RIGHT, more=x[h][0])
+        part(h, RIGHT, r[h].at[core], 2 * after)
 
     def collect(h):
         wait(r[h], r_recv.at[h])
-        nothing = jnp.zeros((BLOCK, 2 * WIDTH), jnp.float32)
         for source in (0, 1):
             own = jnp.where(core == source, s[h][own_rows, :].astype(jnp.float32),
                             r[h][4].astype(jnp.float32))
-            far = r[h][5, pl.ds(source * BLOCK, BLOCK)].astype(jnp.float32)
-            far = jnp.concatenate(
-                [jnp.where(core == 0, far, nothing), jnp.where(core == 1, far, nothing)], axis=0
-            )
             total = own + r[h][source].astype(jnp.float32) + r[h][2 + source].astype(jnp.float32)
-            total = (total + far).astype(jnp.bfloat16)
+            total = total.astype(jnp.bfloat16)
             at = pl.ds((HEADS * source + h) * WIDTH, WIDTH)
             dk_out[:, at] = total[:, :WIDTH]
             dv_out[:, at] = total[:, WIDTH:]
@@ -270,6 +273,7 @@
         tiles(h)
         send_partials(h)
         outputs(h)
+        send_edges(h)
         send_outputs(h)
     for i, dst in enumerate((o_hbm, dq_hbm)):
         near(od.at[i, token_rows], dst.at[:, mine], o_own)
@@ -282,6 +286,7 @@
     wait(kv[HEADS - 1].at[:, : WINDOW - 2], kv_send.at[HEADS - 1])
     for h in range(HEADS):
         wait(r[h], r_send.at[h])
+        wait(x[h], x_send.at[h])
     wait(qg_in, qg_send)
     wait(od_far, o_send)
     wait(od_far, o_own)
@@ -339,11 +344,12 @@
             pltpu.VMEM((CHIP_BLOCKS, REACH + 2, BLOCK, 2 * WIDTH), jnp.float32),
             *some(2, (CHIP_BLOCKS, SPAN, half // HEADS // WIDTH * BLOCK)),
             *some(HEADS, (WINDOW * BLOCK, 2 * WIDTH)),
-            *some(HEADS, (6, local, 2 * WIDTH)),
+            *some(HEADS, (2, BLOCK, 2 * WIDTH)),
+            *some(HEADS, (5, local, 2 * WIDTH)),
             pltpu.SMEM((CHIP_BLOCKS,), jnp.int32),
             pltpu.SMEM((CHIP_BLOCKS,), jnp.int32),
             dma((2,)), dma, dma, dma((HEADS,)), dma((HEADS,)), dma, dma((HEADS,)),
-            dma((HEADS,)), dma((HEADS,)), dma, dma, dma, dma,
+            dma((HEADS,)), dma((HEADS, 2)), dma((HEADS,)), dma((HEADS,)), dma, dma, dma, dma,
         ],
         compiler_params=pltpu.CompilerParams(
             collective_id=0, has_side_effects=True, vmem_limit_bytes=56 * 2**20

time: 35.3 us -> 37.4 us (1.059)
  Pallas kernels: 34.5 us -> 36.6 us
    pallas_call x1, Pallas kernels: 32.1 us -> 34.2 us  [per_device(): pl.pallas_call(kernel, out_shape=shapes, in_specs=[whole] * 4 + [scalars]...]
where the time goes in v6:
time: 37.4 us; the launch traced here: 37.2 us
  Pallas kernels  36.6 us (98%)
  between operations  0.64 us (2%)
    pallas_call x1, Pallas kernels, per_device(): pl.pallas_call(kernel, out_shape=shapes, in_specs=[whole] * 4 + [scalars]...  34.2 us
    pallas_call x1, Pallas kernels, per_device(): pl.pallas_call(settle, out_shape=shapes, in_specs=[pl.BlockSpec(memory_sp...  2.35 us

profile of v6, /device:TPU:1, one launch (start us, length us, event | category | flops | bytes accessed | tf_op | source)
XLA Modules:
  0.0 37.2 jit_solution(17436443702594059845)
XLA Ops:
  0.6 34.2 %shard_map.93 = (bf16[128,3072]{1,0:T(8,128)(2,1)}, bf16[128,3072]{1,0:T(8,128)(2,1)}, bf16[128,512]{1,0:T(8,128)(2,1)}, bf16[128,512]{1,0:T(8,128)(2,1)}) custom-call(bf16[128,3072]{1,0:T(8,128)(2,1)} %q_hbm.1, bf16[2,64,512]{2,1,0:T(8,128)(2,1)} %bitcast.2, bf16[2,64,512]{2,1,0:T(8,128)(2,1)} %bitcast.3, bf16[128,3072]{1,0:T(8,128)(2,1)} %g_hbm.1, ...), custom_call_target="tpu_custom_call" | custom-call | flops 1811939328 | bytes 3670016 | tf_op jit(solution)/shard_map/pallas_call | solution.py:331
  34.8 2.4 %shard_map.94 = (bf16[128,3072]{1,0:T(8,128)(2,1)}, bf16[128,3072]{1,0:T(8,128)(2,1)}, bf16[128,512]{1,0:T(8,128)(2,1)}, bf16[128,512]{1,0:T(8,128)(2,1)}) custom-call(bf16[128,3072]{1,0:T(8,128)(2,1)} %get-tuple-element.8.refs_0_, bf16[128,3072]{1,0:T(8,128)(2,1)} %get-tuple-element.9.refs_1_, bf16[128,512]{1,0:T(8,128)(2,1)} %get-tuple-element.10.refs_2_, ...), custom_call_target="tpu_custom_call" | custom-call | tf_op jit(solution)/shard_map/pallas_call | solution.py:370

commit v7 on v5

--- a/solution.py
+++ b/solution.py
@@ -17,7 +17,6 @@
 HEADS = 2
 SPAN = REACH * BLOCK
 PIECES = 2
-ORDER = (0, 3, 1, 2)
 LOG2E = 1.4426950408889634
 
 
@@ -97,9 +96,19 @@
     across = (((1,), (1,)), ((), ()))
     down = (((0,), (0,)), ((), ()))
 
+    def tokens_of(t):
+        return pl.ds(pl.multiple_of(t * BLOCK, BLOCK), BLOCK)
+
+    def each_block(work):
+        def step(t, carry):
+            work(t)
+            return carry
+
+        lax.fori_loop(0, CHIP_BLOCKS, step, 0)
+
     def load(h, t):
         begin = first[t]
-        tokens = pl.ds(t * BLOCK, BLOCK)
+        tokens = tokens_of(t)
 
         def windowed(kind):
             return jnp.concatenate([kv[h][kind, begin + b] for b in range(REACH)], axis=0)
@@ -150,21 +159,13 @@
             parts[t, b + 1, :, WIDTH:] = dvalues[at]
 
     def tiles(h):
-        made = products(h, ORDER[0])
-        for i, t in enumerate(ORDER):
-            ready = made
-            if i + 1 < CHIP_BLOCKS:
-                made = products(h, ORDER[i + 1])
-            finish(h, t, *softmax(t, *ready))
-            if t == 0:
-                put_sums(h, 0)
-                part(h, 0, 1, far_slot(h), 2 * before2 + 1)
-            if t == CHIP_BLOCKS - 1:
-                put_sums(h, WINDOW - 1)
-                part(h, WINDOW - 1, 1, far_slot(h), 2 * after2)
+        each_block(lambda t: finish(h, t, *softmax(t, *products(h, t))))
+        put_sums(h, 0, WINDOW - 1)
+        part(h, 0, 1, far_slot(h), 2 * before2 + 1)
+        part(h, WINDOW - 1, 1, far_slot(h), 2 * after2)
 
     def outputs(h):
-        for t in range(CHIP_BLOCKS):
+        def work(t):
             keys, values, _, _ = load(h, t)
             attn = lax.dot_general(values, low_held[t], down, preferred_element_type=jnp.float32)
             dquery = lax.dot_general(keys, dlow_held[t], down, preferred_element_type=jnp.float32)
@@ -172,9 +173,10 @@
             dquery = (dquery * score_scale).astype(jnp.bfloat16).T
             for m in range(group):
                 at = pl.ds(h * cols + m * WIDTH, WIDTH)
-                tokens = pl.ds(t * BLOCK, BLOCK)
-                od[0, tokens, at] = attn[m * BLOCK : (m + 1) * BLOCK]
-                od[1, tokens, at] = dquery[m * BLOCK : (m + 1) * BLOCK]
+                od[0, tokens_of(t), at] = attn[m * BLOCK : (m + 1) * BLOCK]
+                od[1, tokens_of(t), at] = dquery[m * BLOCK : (m + 1) * BLOCK]
+
+        each_block(work)
 
     scale_row = jnp.where(
         lax.broadcasted_iota(jnp.int32, (1, 2 * WIDTH), 1) < WIDTH, score_scale, 1.0

time: 35.3 us -> 37 us (1.048)
  Pallas kernels: 34.5 us -> 36.2 us
    pallas_call x1, Pallas kernels: 32.1 us -> 33.8 us  [per_device(): pl.pallas_call(kernel, out_shape=shapes, in_specs=[whole] * 4 + [scalars]...]
where the time goes in v7:
time: 37 us; the launch traced here: 36.8 us
  Pallas kernels  36.2 us (98%)
  between operations  0.64 us (2%)
    pallas_call x1, Pallas kernels, per_device(): pl.pallas_call(kernel, out_shape=shapes, in_specs=[whole] * 4 + [scalars]...  33.8 us
    pallas_call x1, Pallas kernels, per_device(): pl.pallas_call(settle, out_shape=shapes, in_specs=[pl.BlockSpec(memory_sp...  2.35 us

profile of v7, /device:TPU:1, one launch (start us, length us, event | category | flops | bytes accessed | tf_op | source)
XLA Modules:
  0.0 36.8 jit_solution(3745952091213396420)
XLA Ops:
  0.6 33.8 %shard_map.93 = (bf16[128,3072]{1,0:T(8,128)(2,1)}, bf16[128,3072]{1,0:T(8,128)(2,1)}, bf16[128,512]{1,0:T(8,128)(2,1)}, bf16[128,512]{1,0:T(8,128)(2,1)}) custom-call(bf16[128,3072]{1,0:T(8,128)(2,1)} %q_hbm.1, bf16[2,64,512]{2,1,0:T(8,128)(2,1)} %bitcast.2, bf16[2,64,512]{2,1,0:T(8,128)(2,1)} %bitcast.3, bf16[128,3072]{1,0:T(8,128)(2,1)} %g_hbm.1, ...), custom_call_target="tpu_custom_call" | custom-call | flops 1811939328 | bytes 3670016 | tf_op jit(solution)/shard_map/pallas_call | solution.py:328
  34.4 2.4 %shard_map.94 = (bf16[128,3072]{1,0:T(8,128)(2,1)}, bf16[128,3072]{1,0:T(8,128)(2,1)}, bf16[128,512]{1,0:T(8,128)(2,1)}, bf16[128,512]{1,0:T(8,128)(2,1)}) custom-call(bf16[128,3072]{1,0:T(8,128)(2,1)} %get-tuple-element.8.refs_0_, bf16[128,3072]{1,0:T(8,128)(2,1)} %get-tuple-element.9.refs_1_, bf16[128,512]{1,0:T(8,128)(2,1)} %get-tuple-element.10.refs_2_, ...), custom_call_target="tpu_custom_call" | custom-call | tf_op jit(solution)/shard_map/pallas_call | solution.py:366
